TPU v7x, 256 devices: a whole 4x4x8 slice. The times are simulated.
256 devices in a mesh: ctx: 32 (over x, y, core), grp: 8 (over z).
Axes of the slice: x: 4, y: 4, z: 8, core: 2. Of those that a mesh axis runs over, the one named last changes fastest.
Arguments:
- tokens: bfloat16 [8, 20480, 768], P('grp', 'ctx'), may hold values from -48 to 48
- slot_query: bfloat16 [768, 1024], replicated, may hold values from -0.4330127 to 0.4330127
- expert_in: bfloat16 [256, 768, 3072], P(('ctx', 'grp')), may hold values from -1.796875 to 1.796875
- expert_out: bfloat16 [256, 3072, 768], P(('ctx', 'grp')), may hold values from -0.47851562 to 0.47851562
Outputs:
- mixed: bfloat16 [8, 20480, 768], P('grp', 'ctx')
All inputs are finite; a program needn't handle non-finite values.
Results may differ from a plain program's by a relative error of at most 0.015.
Values may be sent and summed in bfloat16 or wider, within the bound.
No kernel may reach another device: no remote copies, remote signals or barrier semaphores. Data moves between devices by JAX's collectives and lax.ppermute only.
A program may use at most 64 MiB of HBM per device.

v0:
```python
import jax
import jax.numpy as jnp
from jax import lax
from jax.sharding import PartitionSpec as P


def per_device(tokens, slot_query, expert_in, expert_out):
    local_tokens = tokens[0]
    logits = jnp.dot(local_tokens, slot_query, preferred_element_type=jnp.float32)
    column_max = lax.pmax(jnp.max(logits, axis=0), "ctx")
    scaled = jnp.exp(logits - column_max[None, :])
    denominator = lax.psum(jnp.sum(scaled, axis=0), "ctx")
    dispatch = (scaled / denominator[None, :]).astype(jnp.bfloat16)
    ctx_count = lax.axis_size("ctx")
    grp_count = lax.axis_size("grp")
    slot_rows = dispatch.shape[1] // ctx_count
    partial_sums = lax.dot_general(
        dispatch, local_tokens, (((0,), (0,)), ((), ())), preferred_element_type=jnp.float32
    )
    summed = lax.psum(partial_sums.astype(jnp.bfloat16), "ctx").astype(jnp.float32)
    owned_rows = lax.dynamic_slice_in_dim(summed, lax.axis_index("ctx") * slot_rows, slot_rows, 0)
    width = local_tokens.shape[1]
    slot_inputs = owned_rows.astype(jnp.bfloat16).reshape(grp_count, slot_rows // grp_count, width)
    received = lax.all_to_all(slot_inputs, "grp", split_axis=0, concat_axis=0, tiled=True)
    flat_rows = received.reshape(-1, width)
    hidden = jax.nn.gelu(
        jnp.dot(flat_rows, expert_in[0], preferred_element_type=jnp.float32), approximate=True
    ).astype(jnp.bfloat16)
    produced = jnp.dot(hidden, expert_out[0], preferred_element_type=jnp.float32).astype(
        jnp.bfloat16
    )
    returned = lax.all_to_all(
        produced.reshape(received.shape), "grp", split_axis=0, concat_axis=0, tiled=True
    )
    slot_outputs = returned.reshape(slot_rows, width)
    row_max = jnp.max(logits, axis=1, keepdims=True)
    row_scaled = jnp.exp(logits - row_max)
    combine_weights = (row_scaled / jnp.sum(row_scaled, axis=1, keepdims=True)).astype(jnp.bfloat16)
    mixed = jnp.dot(
        combine_weights,
        lax.all_gather(slot_outputs, "ctx", axis=0, tiled=True),
        preferred_element_type=jnp.float32,
    )
    return mixed.astype(jnp.bfloat16)[None]


def solution(mesh):
    in_specs = (
        P("grp", "ctx", None),
        P(),
        P(("ctx", "grp"), None, None),
        P(("ctx", "grp"), None, None),
    )
    out_specs = P("grp", "ctx", None)
    return jax.shard_map(
        per_device, mesh=mesh, in_specs=in_specs, out_specs=out_specs, check_vma=False
    )
```

profile of v0, /device:TPU:1, one launch (start us, length us, event | category | flops | bytes accessed | tf_op | source)
XLA Modules:
  0.0 351.1 jit_solution(14177342731569649296)
XLA Ops:
  6.5 0.0 copy-start
  6.5 0.0 all-reduce.2.cloned.1.call-start
  6.5 1.4 copy-done
  7.9 3.9 %fusion.36 = (f32[640]{0:T(1024)S(1)}, f32[1024]{0:T(1024)S(1)}, f32[640,1024]{1,0:T(8,128)}) fusion(bf16[768,1024]{1,0:T(8,128)(2,1)S(1)} %copy-done, bf16[1,640,768]{2,1,0:T(8,128)(2,1)} %param.4), kind=kOutput, calls=%fused_computation.36 | convolution fusion | flops 1007942016 | bytes 5184000 | tf_op jit(solution)/shard_map/dot_general | solution.py:9
  11.8 0.0 copy-start.1
  11.8 65.4 %pmax.7 = f32[1024]{0:T(1024)S(1)} all-reduce(f32[1024]{0:T(1024)S(1)} %get-tuple-element.8), channel_id=1, replica_groups=mesh['ctx'=32,'grp'=8] {'ctx'}, use_global_device_ids=true, to_apply=%region_3.0 | all-reduce | flops 1024 | bytes 8192 | tf_op jit(solution)/shard_map/pmax | solution.py:10
  77.2 2.7 fusion.4
  79.9 65.6 %psum.14 = f32[1024]{0:T(1024)S(1)} all-reduce(f32[1024]{0:T(1024)S(1)} %get-tuple-element.6), channel_id=1, replica_groups=mesh['ctx'=32,'grp'=8] {'ctx'}, use_global_device_ids=true, to_apply=%region_5.0 | all-reduce | flops 1024 | bytes 8192 | tf_op jit(solution)/shard_map/psum | solution.py:12
  145.5 0.0 copy-done.1
  145.5 4.4 %convolution_convert_fusion = bf16[1024,768]{1,0:T(8,128)(2,1)} fusion(f32[640,1024]{1,0:T(8,128)} %get-tuple-element.9, f32[1024]{0:T(1024)S(1)} %psum.14, f32[1024]{0:T(1024)S(1)} %pmax.7, bf16[1,640,768]{2,1,0:T(8,128)(2,1)S(1)} %copy-done.1), kind=kOutput, calls=%fused_computation.10 | convolution fusion | flops 1009385472 | bytes 5185536 | tf_op jit(solution)/shard_map/dot_general | solution.py:17
  149.9 0.0 all-reduce.2.cloned.1.call-update
  149.9 0.0 all-gather.2.cloned.1.call-start
  149.9 114.0 %all-reduce.2.cloned.1.call-done = bf16[1024,768]{1,0:T(8,128)(2,1)} async-done(((bf16[1024,768]{1,0:T(8,128)(2,1)}), bf16[1024,768]{1,0:T(8,128)(2,1)}) %all-reduce.2.cloned.1.call-update) | async-done | bytes 1572880 | tf_op jit(solution)/shard_map/psum | solution.py:20
  264.0 0.8 convert_convert_fusion
  264.8 13.6 %all_to_all.10 = bf16[8,4,768]{2,1,0:T(4,128)(2,1)S(1)} all-to-all(bf16[8,4,768]{2,1,0:T(4,128)(2,1)S(1)} %reshape.16), channel_id=1, replica_groups=mesh['ctx'=32,'grp'=8] {'grp'}, dimensions={0} | all-to-all | bytes 98304 | tf_op jit(solution)/shard_map/all_to_all | solution.py:24
  278.4 5.5 %fusion.8 = bf16[32,768]{1,0:T(8,128)(2,1)S(1)} fusion(bf16[1,3072,768]{2,1,0:T(8,128)(2,1)} %param.7, bf16[32,768]{1,0:T(8,128)(2,1)S(1)} %reshape.17, bf16[1,768,3072]{2,1,0:T(8,128)(2,1)} %param.6), kind=kOutput, calls=%fused_computation.14 | convolution fusion | flops 302899200 | bytes 9535488 | tf_op jit(solution)/shard_map/dot_general | solution.py:29
  284.0 9.4 %all_to_all.11 = bf16[8,4,768]{2,1,0:T(4,128)(2,1)S(1)} all-to-all(bf16[8,4,768]{2,1,0:T(4,128)(2,1)S(1)} %reshape.18), channel_id=1, replica_groups=mesh['ctx'=32,'grp'=8] {'grp'}, dimensions={0} | all-to-all | bytes 98304 | tf_op jit(solution)/shard_map/all_to_all | solution.py:32
  293.4 0.6 reshape.19
  294.0 0.0 all-gather.2.cloned.1.call-update
  294.1 45.7 %all-gather.2.cloned.1.call-done = bf16[1024,768]{1,0:T(8,128)(2,1)} async-done(((bf16[32,768]{1,0:T(8,128)(2,1)}), bf16[1024,768]{1,0:T(8,128)(2,1)}) %all-gather.2.cloned.1.call-update) | async-done | bytes 1572880 | tf_op jit(solution)/shard_map/all_gather | solution.py:41
  339.8 4.4 %fusion.6 = bf16[1,640,768]{2,1,0:T(8,128)(2,1)} fusion(bf16[1024,768]{1,0:T(8,128)(2,1)} %all-gather.2.cloned.1.call-done, f32[640,1024]{1,0:T(8,128)} %get-tuple-element.9, f32[640]{0:T(1024)S(1)} %get-tuple-element.5, f32[640]{0:T(1024)S(1)} %get-tuple-element.7), kind=kOutput, calls=%fused_computation.12 | convolution fusion | flops 1009090560 | bytes 5182464 | tf_op jit(solution)/shard_map/dot_general | solution.py:39
  (3 shorter events, 0.1 us)
Async XLA Ops:
  6.5 1.4 copy-start
  6.5 257.5 %all-reduce.2.cloned.1.call-start = ((), (), s32[]{:S(2)}) async-start(), calls=%async_computation.2 | async-start | bytes 3145728 | tf_op jit(solution)/shard_map/psum | solution.py:20
  11.8 133.6 %copy-start.1 = (bf16[1,640,768]{2,1,0:T(8,128)(2,1)S(1)}, bf16[1,640,768]{2,1,0:T(8,128)(2,1)}, u32[]{:S(2)}) copy-start(bf16[1,640,768]{2,1,0:T(8,128)(2,1)} %param.4) | copy-start | bytes 2949124
  149.9 189.9 %all-gather.2.cloned.1.call-start = ((), (), s32[]{:S(2)}) async-start(), calls=%async_computation.3 | async-start | bytes 1622016 | tf_op jit(solution)/shard_map/all_gather | solution.py:41
Sparse Core Ops, SparseCore 0:
  150.0 113.9 all-reduce.1
  294.2 45.5 all-gather.1
where the time goes:
time: 351 us
  waiting for transfers between devices  160 us (46%)
  blocking collectives  154 us (44%)
  matrix products  18.2 us (5%)
  between operations  13.4 us (4%)
    psum x1, waiting for transfers between devices, per_device(): lax.psum(partial_sums.astype(jnp.bfloat16), 'ctx').astype(jnp.float32)  114 us
    psum x1, blocking collectives, per_device(): denominator = lax.psum(jnp.sum(scaled, axis=0), 'ctx')  65.6 us
    pmax x1, blocking collectives, per_device(): column_max = lax.pmax(jnp.max(logits, axis=0), 'ctx')  65.4 us
    all_gather x1, waiting for transfers between devices, per_device(): lax.all_gather(slot_outputs, 'ctx', axis=0, tiled=True)  45.7 us
    all_to_all x1, blocking collectives, per_device(): lax.all_to_all(slot_inputs, 'grp', split_axis=0, concat_axis=0, tiled=True)  13.6 us
    all_to_all x1, blocking collectives, per_device(): lax.all_to_all(produced.reshape(received.shape), 'grp', split_axis=0, con...  9.42 us
  transfers between devices with their start and end apart: 2, of which 2 were waited for; matrix products, arithmetic and copies ran while one was open for 0% of the time, Pallas kernels for 0%

commit v1 on v0

v1 whole, which is shorter than its diff:
```python
import jax
import jax.numpy as jnp
from jax import lax
from jax.sharding import Mesh, PartitionSpec as P

BF16 = jnp.bfloat16
F32 = jnp.float32
SWAP = [(0, 1), (1, 0)]


def pack(sums, peak, total):
    high = lax.reduce_precision(total, 8, 7)
    extra = jnp.stack([peak, high, total - high], axis=1)
    extra = jnp.pad(extra, ((0, 0), (0, 125)))
    return jnp.concatenate([sums.astype(BF16), extra.astype(BF16)], axis=1)


def unpack(rows, width):
    sums = rows[..., :width].astype(F32)
    extra = rows[..., width:width + 3].astype(F32)
    return sums, extra[..., 0], extra[..., 1] + extra[..., 2]


def partial_sums(local_tokens, query):
    logits = jnp.dot(local_tokens, query, preferred_element_type=F32)
    peak = lax.reduce_precision(jnp.max(logits, axis=0), 8, 7)
    scaled = jnp.exp(logits - peak[None, :])
    sums = lax.dot_general(
        scaled.astype(BF16), local_tokens, (((0,), (0,)), ((), ())), preferred_element_type=F32
    )
    return logits, sums, peak, jnp.sum(scaled, axis=0)


def per_device(tokens, slot_query, expert_in, expert_out):
    local_tokens = tokens[0]
    width = local_tokens.shape[1]
    chips = lax.axis_size("x") * lax.axis_size("y")
    grp_count = lax.axis_size("grp")
    slots = slot_query.shape[1]
    slot_rows = slots // (2 * chips)
    core = lax.axis_index("core")
    split = slot_query.reshape(width, chips, 2, slot_rows)
    first = split[:, :, 0].reshape(width, slots // 2)
    second = split[:, :, 1].reshape(width, slots // 2)
    own_query = jnp.where(core == 0, first, second)
    other_query = jnp.where(core == 0, second, first)

    other_logits, sums, peak, total = partial_sums(local_tokens, other_query)
    arrived = lax.ppermute(pack(sums, peak, total), "core", SWAP)
    own_logits, sums, peak, total = partial_sums(local_tokens, own_query)
    sums2, peak2, total2 = unpack(arrived, width)
    top = jnp.maximum(peak, peak2)
    w1, w2 = jnp.exp(peak - top), jnp.exp(peak2 - top)
    sums = sums * w1[:, None] + sums2 * w2[:, None]
    packed = pack(sums, top, total * w1 + total2 * w2)
    parts = lax.all_to_all(
        packed.reshape(chips, slot_rows, -1), ("x", "y"), split_axis=0, concat_axis=0, tiled=True
    )
    sums, peak, total = unpack(parts, width)
    weight = jnp.exp(peak - jnp.max(peak, axis=0))
    slot_inputs = (
        jnp.sum(sums * weight[..., None], axis=0) / jnp.sum(total * weight, axis=0)[:, None]
    ).astype(BF16)

    received = lax.all_to_all(
        slot_inputs.reshape(grp_count, slot_rows // grp_count, width),
        "grp", split_axis=0, concat_axis=0, tiled=True,
    )
    hidden = jax.nn.gelu(
        jnp.dot(received.reshape(-1, width), expert_in[0], preferred_element_type=F32),
        approximate=True,
    ).astype(BF16)
    produced = jnp.dot(hidden, expert_out[0], preferred_element_type=F32).astype(BF16)
    returned = lax.all_to_all(
        produced.reshape(received.shape), "grp", split_axis=0, concat_axis=0, tiled=True
    ).reshape(1, slot_rows, width)
    own = lax.all_to_all(
        jnp.broadcast_to(returned, (chips, slot_rows, width)),
        ("x", "y"), split_axis=0, concat_axis=0, tiled=True,
    ).reshape(slots // 2, width)
    other = lax.ppermute(own, "core", SWAP)

    row_max = jnp.maximum(jnp.max(own_logits, axis=1), jnp.max(other_logits, axis=1))[:, None]
    own_weights = jnp.exp(own_logits - row_max)
    other_weights = jnp.exp(other_logits - row_max)
    row_total = jnp.sum(own_weights, axis=1) + jnp.sum(other_weights, axis=1)
    mixed = jnp.dot(own_weights.astype(BF16), own, preferred_element_type=F32)
    mixed = mixed + jnp.dot(other_weights.astype(BF16), other, preferred_element_type=F32)
    return (mixed / row_total[:, None]).astype(BF16)[None]


def solution(mesh):
    fine = Mesh(mesh.devices.reshape(4, 4, 2, 8), ("x", "y", "core", "grp"))
    ctx = ("x", "y", "core")
    in_specs = (
        P("grp", ctx, None),
        P(),
        P(ctx + ("grp",), None, None),
        P(ctx + ("grp",), None, None),
    )
    return jax.shard_map(
        per_device, mesh=fine, in_specs=in_specs, out_specs=P("grp", ctx, None), check_vma=False
    )
```

time: 351 us -> 87.6 us (0.25)
  waiting for transfers between devices: 160 us -> 3.28 us
  blocking collectives: 154 us -> 57.8 us
  between operations: 13.4 us -> 0.21 us
  starting transfers between devices: 0.04 us -> 8.85 us
  matrix products: 18.2 us -> 11.7 us
    psum x1 -> x0, waiting for transfers between devices: 114 us -> none  [per_device(): lax.psum(partial_sums.astype(jnp.bfloat16), 'ctx').astype(jnp.float32)]
    psum x1 -> x0, blocking collectives: 65.6 us -> none  [per_device(): denominator = lax.psum(jnp.sum(scaled, axis=0), 'ctx')]
    pmax x1 -> x0, blocking collectives: 65.4 us -> none  [per_device(): column_max = lax.pmax(jnp.max(logits, axis=0), 'ctx')]
    all_gather x1 -> x0, waiting for transfers between devices: 45.7 us -> none  [per_device(): lax.all_gather(slot_outputs, 'ctx', axis=0, tiled=True)]
    all_to_all x1 -> x3, blocking collectives: 13.6 us -> 48.3 us  [the longest x1 19.1 us: per_device(): lax.all_to_all(packed.reshape(chips, slot_rows, -1), ('x', 'y'), split_ax...]
    ppermute x0 -> x2, starting transfers between devices: none -> 8.85 us  [the longest x1 5.52 us: per_device(): other = lax.ppermute(own, 'core', SWAP)]
    dot_general x4 -> x7, matrix products: 18.2 us -> 11.7 us  [the longest x1 5.51 us: per_device(): jnp.dot(hidden, expert_out[0], preferred_element_type=F32).astype(BF16)]
  transfers between devices with their start and end apart: 2 -> 2, of which waited for: 2 -> 2; matrix products, arithmetic and copies ran while one was open for 0% -> 1% of each run, Pallas kernels for 0% -> 0%
where the time goes in v1:
time: 87.6 us; the launch traced here: 87.3 us
  blocking collectives  57.8 us (66%)
  matrix products  11.7 us (13%)
  starting transfers between devices  8.85 us (10%)
  local copies, waits for them, and re-layouts  3.52 us (4%)
  waiting for transfers between devices  3.28 us (4%)
  other arithmetic  1.96 us (2%)
    all_to_all x1, blocking collectives, per_device(): lax.all_to_all(packed.reshape(chips, slot_rows, -1), ('x', 'y'), split_ax...  19.1 us
    all_to_all x1, blocking collectives, per_device(): lax.all_to_all(slot_inputs.reshape(grp_count, slot_rows // grp_count, wid...  15.1 us
    all_to_all x1, blocking collectives, per_device(): lax.all_to_all(jnp.broadcast_to(returned, (chips, slot_rows, width)), ('x...  14.1 us
    all_to_all x1, blocking collectives, per_device(): lax.all_to_all(produced.reshape(received.shape), 'grp', split_axis=0, con...  9.42 us
    ppermute x1, starting transfers between devices, per_device(): other = lax.ppermute(own, 'core', SWAP)  5.52 us
    dot_general x1, matrix products, per_device(): jnp.dot(hidden, expert_out[0], preferred_element_type=F32).astype(BF16)  5.51 us
    ppermute x1, starting transfers between devices, per_device(): arrived = lax.ppermute(pack(sums, peak, total), 'core', SWAP)  3.33 us
    ppermute x1, waiting for transfers between devices, per_device(): arrived = lax.ppermute(pack(sums, peak, total), 'core', SWAP)  2.1 us
  transfers between devices with their start and end apart: 2, of which 2 were waited for; matrix products, arithmetic and copies ran while one was open for 1% of the time, Pallas kernels for 0%

profile of v1, /device:TPU:1, one launch (start us, length us, event | category | flops | bytes accessed | tf_op | source)
XLA Modules:
  0.0 87.3 jit_solution(294136567329016618)
XLA Ops:
  0.0 0.0 copy-start
  0.0 1.8 %copy.52 = bf16[768,1024]{0,1:T(8,128)(2,1)S(1)} copy(bf16[768,1024]{1,0:T(8,128)(2,1)} %param.5) | data formatting | bytes 3145728 | tf_op args[1]
  1.8 0.1 broadcast_select_fusion.1
  1.9 0.0 copy-done
  1.9 0.9 %fusion.77 = (f32[640]{0:T(1024)S(1)}, f32[512]{0:T(512)S(1)}, f32[512,640]{1,0:T(8,128)S(1)}) fusion(bf16[768,512]{0,1:T(8,128)(2,1)S(1)} %bitcast.65, bf16[1,640,768]{2,1,0:T(8,128)(2,1)S(1)} %copy-done), kind=kOutput, calls=%fused_computation.90 | convolution fusion | flops 503970688 | bytes 3084800 | tf_op jit(solution)/shard_map/dot_general | solution.py:25
  2.8 0.0 copy-start.1
  2.9 0.9 %fusion.78 = (f32[640]{0:T(1024)S(1)}, f32[512]{0:T(512)S(1)}, f32[512,640]{1,0:T(8,128)S(1)}) fusion(bf16[768,512]{0,1:T(8,128)(2,1)S(1)} %bitcast.64, bf16[1,640,768]{2,1,0:T(8,128)(2,1)S(1)} %copy-done), kind=kOutput, calls=%fused_computation.91 | convolution fusion | flops 503970688 | bytes 3084800 | tf_op jit(solution)/shard_map/dot_general | solution.py:25
  3.8 1.0 %convolution_convert_fusion = bf16[512,768]{0,1:T(8,128)(2,1)S(1)} fusion(bf16[1,640,768]{2,1,0:T(8,128)(2,1)S(1)} %copy-done, f32[512,640]{1,0:T(8,128)S(1)} %get-tuple-element.25, f32[512]{0:T(512)S(1)} %get-tuple-element.22), kind=kOutput, calls=%fused_computation.7 | convolution fusion | flops 504365056 | bytes 3082240 | tf_op jit(solution)/shard_map/dot_general | solution.py:28
  4.8 0.0 copy-done.1
  4.8 1.3 %fusion.11 = (f32[640]{0:T(1024)S(1)}, f32[512]{0:T(512)S(1)}, f32[512]{0:T(512)S(1)}, f32[640]{0:T(1024)S(1)}) fusion(f32[512,640]{1,0:T(8,128)S(1)} %get-tuple-element.25, f32[640]{0:T(1024)S(1)} %max.15, f32[512]{0:T(512)S(1)} %get-tuple-element.22, f32[512,640]{1,0:T(8,128)S(1)} %get-tuple-element.26, f32[512]{0:T(512)S(1)} %reduce_precision.57), kind=kLoop, calls=%fused_computation.19 | loop fusion | flops 2619136 | bytes 2637312 | tf_op jit(solution)/shard_map/reduce_sum | solution.py:86
  6.1 0.1 pad_maximum_fusion
  6.1 3.3 %collective-permute-start = (bf16[512,896]{0,1:T(8,128)(2,1)S(1)}, bf16[512,896]{0,1:T(8,128)(2,1)S(1)}, u32[]{:S(2)}, u32[]{:S(2)}) collective-permute-start(bf16[512,896]{0,1:T(8,128)(2,1)S(1)} %pad_maximum_fusion), channel_id=1, source_target_pairs={{0,8},{8,0},{1,9},{9,1},{2,10},{10,2},{3,11},{11,3},{4,12},{12,4},... | collective-permute-start | bytes 2752520 | tf_op jit(solution)/shard_map/ppermute | solution.py:49
  9.5 2.1 %collective-permute-done = bf16[512,896]{0,1:T(8,128)(2,1)S(1)} collective-permute-done((bf16[512,896]{0,1:T(8,128)(2,1)S(1)}, bf16[512,896]{0,1:T(8,128)(2,1)S(1)}, u32[]{:S(2)}, u32[]{:S(2)}) %collective-permute-start) | collective-permute-done | bytes 917536 | tf_op jit(solution)/shard_map/ppermute | solution.py:49
  11.6 1.0 %add_convert_fusion = bf16[512,768]{0,1:T(8,128)(2,1)S(1)} fusion(bf16[512,896]{0,1:T(8,128)(2,1)S(1)} %collective-permute-done, f32[512]{0:T(512)S(1)} %bitcast.71, f32[512]{0:T(512)S(1)} %bitcast.70, bf16[1,640,768]{2,1,0:T(8,128)(2,1)S(1)} %copy-done, f32[512,640]{1,0:T(8,128)S(1)} %get-tuple-element.26, f32[512]{0:T(512)S(1)} %reduce_precision.57), kind=kOutput, calls=%fused_computation.6 | convolution fusion | flops 505937920 | bytes 3872768 | tf_op jit(solution)/shard_map/dot_general | solution.py:28
  12.6 0.1 pad_maximum_fusion.1
  12.7 1.3 %copy.55 = bf16[512,896]{1,0:T(8,128)(2,1)} copy(bf16[512,896]{0,1:T(8,128)(2,1)S(1)} %pad_maximum_fusion.1) | data formatting | bytes 1835008 | tf_op jit(solution)/shard_map/concatenate | solution.py:15
  14.0 19.1 %all_to_all.20 = bf16[16,32,896]{2,1,0:T(8,128)(2,1)S(1)} all-to-all(bf16[16,32,896]{2,1,0:T(8,128)(2,1)} %bitcast.61), channel_id=1, replica_groups=mesh['x'=4,'y'=4,'core'=2,'grp'=8] {'x','y'}, dimensions={0} | all-to-all | bytes 1835008 | tf_op jit(solution)/shard_map/all_to_all | solution.py:56
  33.1 0.2 copy.62
  33.4 0.2 multiply_reduce_fusion
  33.6 0.1 div.19
  33.7 0.1 divide_convert_fusion.1
  33.8 15.1 %all_to_all.21 = bf16[8,4,768]{2,1,0:T(4,128)(2,1)S(1)} all-to-all(bf16[8,4,768]{2,1,0:T(4,128)(2,1)S(1)} %divide_convert_fusion.1), channel_id=1, replica_groups=mesh['x'=4,'y'=4,'core'=2,'grp'=8] {'grp'}, dimensions={0} | all-to-all | bytes 98304 | tf_op jit(solution)/shard_map/all_to_all | solution.py:65
  49.0 5.5 %fusion.13 = bf16[32,768]{1,0:T(8,128)(2,1)S(1)} fusion(bf16[1,3072,768]{2,1,0:T(8,128)(2,1)} %param.7, bf16[32,768]{1,0:T(8,128)(2,1)S(1)} %reshape.89, bf16[1,768,3072]{2,1,0:T(8,128)(2,1)} %param.6), kind=kOutput, calls=%fused_computation.21 | convolution fusion | flops 302899200 | bytes 9535488 | tf_op jit(solution)/shard_map/dot_general | solution.py:73
  54.5 9.4 %all_to_all.22 = bf16[8,4,768]{2,1,0:T(4,128)(2,1)S(1)} all-to-all(bf16[8,4,768]{2,1,0:T(4,128)(2,1)S(1)} %reshape.90), channel_id=1, replica_groups=mesh['x'=4,'y'=4,'core'=2,'grp'=8] {'grp'}, dimensions={0} | all-to-all | bytes 98304 | tf_op jit(solution)/shard_map/all_to_all | solution.py:74
  64.0 0.1 broadcast_in_dim.7
  64.0 14.1 %all_to_all.23 = bf16[16,32,768]{2,1,0:T(8,128)(2,1)S(1)} all-to-all(bf16[16,32,768]{2,1,0:T(8,128)(2,1)S(1)} %broadcast_in_dim.7), channel_id=1, replica_groups=mesh['x'=4,'y'=4,'core'=2,'grp'=8] {'x','y'}, dimensions={0} | all-to-all | bytes 1572864 | tf_op jit(solution)/shard_map/all_to_all | solution.py:77
  78.2 5.5 %collective-permute-start.1 = (bf16[512,768]{1,0:T(8,128)(2,1)S(1)}, bf16[512,768]{1,0:T(8,128)(2,1)S(1)}, u32[]{:S(2)}, u32[]{:S(2)}) collective-permute-start(bf16[512,768]{1,0:T(8,128)(2,1)S(1)} %bitcast.62), channel_id=1, source_target_pairs={{0,8},{8,0},{1,9},{9,1},{2,10},{10,2},{3,11},{11,3},{4,12},{12,4},... | collective-permute-start | bytes 2359304 | tf_op jit(solution)/shard_map/ppermute | solution.py:81
  83.7 0.0 copy-start.2
  83.7 0.7 fusion.30
  84.4 1.2 %collective-permute-done.1 = bf16[512,768]{1,0:T(8,128)(2,1)S(1)} collective-permute-done((bf16[512,768]{1,0:T(8,128)(2,1)S(1)}, bf16[512,768]{1,0:T(8,128)(2,1)S(1)}, u32[]{:S(2)}, u32[]{:S(2)}) %collective-permute-start.1) | collective-permute-done | bytes 786464 | tf_op jit(solution)/shard_map/ppermute | solution.py:81
  85.6 0.0 copy-done.2
  85.6 1.7 %fusion.4 = bf16[1,640,768]{2,1,0:T(8,128)(2,1)} fusion(f32[640,768]{1,0:T(8,128)S(1)} %fusion.30, bf16[512,768]{1,0:T(8,128)(2,1)S(1)} %collective-permute-done.1, f32[640]{0:T(1024)S(1)} %add.51, f32[512,640]{1,0:T(8,128)S(1)} %copy-done.2, f32[640]{0:T(1024)S(1)} %max.15), kind=kOutput, calls=%fused_computation.8 | convolution fusion | flops 505446400 | bytes 5051392 | tf_op jit(solution)/shard_map/dot_general | solution.py:88
  (21 shorter events, 0.3 us)
Async XLA Ops:
  0.0 1.9 %copy-start = (bf16[1,640,768]{2,1,0:T(8,128)(2,1)S(1)}, bf16[1,640,768]{2,1,0:T(8,128)(2,1)}, u32[]{:S(2)}) copy-start(bf16[1,640,768]{2,1,0:T(8,128)(2,1)} %param.4) | copy-start | bytes 2949124
  2.8 1.9 %copy-start.1 = (f32[512,640]{1,0:T(8,128)}, f32[512,640]{1,0:T(8,128)S(1)}, u32[]{:S(2)}) copy-start(f32[512,640]{1,0:T(8,128)S(1)} %get-tuple-element.25) | copy-start | bytes 3932164
  6.1 5.4 %collective-permute-start = (bf16[512,896]{0,1:T(8,128)(2,1)S(1)}, bf16[512,896]{0,1:T(8,128)(2,1)S(1)}, u32[]{:S(2)}, u32[]{:S(2)}) collective-permute-start(bf16[512,896]{0,1:T(8,128)(2,1)S(1)} %pad_maximum_fusion), channel_id=1, source_target_pairs={{0,8},{8,0},{1,9},{9,1},{2,10},{10,2},{3,11},{11,3},{4,12},{12,4},... | collective-permute-start | bytes 2752520 | tf_op jit(solution)/shard_map/ppermute | solution.py:49
  78.2 7.4 %collective-permute-start.1 = (bf16[512,768]{1,0:T(8,128)(2,1)S(1)}, bf16[512,768]{1,0:T(8,128)(2,1)S(1)}, u32[]{:S(2)}, u32[]{:S(2)}) collective-permute-start(bf16[512,768]{1,0:T(8,128)(2,1)S(1)} %bitcast.62), channel_id=1, source_target_pairs={{0,8},{8,0},{1,9},{9,1},{2,10},{10,2},{3,11},{11,3},{4,12},{12,4},... | collective-permute-start | bytes 2359304 | tf_op jit(solution)/shard_map/ppermute | solution.py:81
  83.7 1.9 %copy-start.2 = (f32[512,640]{1,0:T(8,128)S(1)}, f32[512,640]{1,0:T(8,128)}, u32[]{:S(2)}) copy-start(f32[512,640]{1,0:T(8,128)} %copy-done.1) | copy-start | bytes 3932164

commit v2 on v1

v2 whole, which is shorter than its diff:
```python
import jax
import jax.numpy as jnp
from jax import lax
from jax.experimental import pallas as pl
from jax.experimental.pallas import tpu as pltpu
from jax.sharding import Mesh, PartitionSpec as P

BF16 = jnp.bfloat16
F32 = jnp.float32
SWAP = [(0, 1), (1, 0)]
LIMIT = 24 * 1024 * 1024
EXTRA = 128
TRANSPOSED = (((1,), (1,)), ((), ()))


def dot(a, b, dims=(((1,), (0,)), ((), ()))):
    return lax.dot_general(a, b, dims, preferred_element_type=F32)


def call(body, outs, flops, moved, *args):
    return pl.pallas_call(
        body,
        out_shape=outs,
        in_specs=[pl.BlockSpec(memory_space=pltpu.VMEM)] * len(args),
        out_specs=[pl.BlockSpec(memory_space=pltpu.VMEM)] * len(outs),
        compiler_params=pltpu.CompilerParams(vmem_limit_bytes=LIMIT),
        cost_estimate=pl.CostEstimate(flops=flops, bytes_accessed=moved, transcendentals=0),
    )(*args)


def row_kernel(own_q, other_q, x, own_logits, own_w, other_w):
    tokens = x[...]
    own = dot(own_q[...], tokens, TRANSPOSED)
    other = dot(other_q[...], tokens, TRANSPOSED)
    own_logits[...] = own
    top = jnp.maximum(jnp.max(own, axis=0, keepdims=True), jnp.max(other, axis=0, keepdims=True))
    own = jnp.exp(own - top)
    other = jnp.exp(other - top)
    total = jnp.sum(own, axis=0, keepdims=True) + jnp.sum(other, axis=0, keepdims=True)
    scale = 1.0 / total
    own_w[...] = (own * scale).astype(BF16)
    other_w[...] = (other * scale).astype(BF16)


def column_kernel(own_q, logits, x, x2, out):
    slots, width = own_q.shape
    block = 128
    lane = lax.broadcasted_iota(jnp.int32, (block, EXTRA), 1)
    for start in range(0, slots, block):
        rows = slice(start, start + block)
        first = logits[rows, :]
        second = dot(own_q[rows, :], x2[...], TRANSPOSED)
        top = jnp.maximum(
            jnp.max(first, axis=1, keepdims=True), jnp.max(second, axis=1, keepdims=True)
        )
        top = top.astype(BF16).astype(F32)
        first = jnp.exp(first - top)
        second = jnp.exp(second - top)
        total = jnp.sum(first, axis=1, keepdims=True) + jnp.sum(second, axis=1, keepdims=True)
        high = total.astype(BF16).astype(F32)
        sums = dot(first.astype(BF16), x[...]) + dot(second.astype(BF16), x2[...])
        out[rows, :width] = sums.astype(BF16)
        extra = jnp.where(lane == 0, top, jnp.where(lane == 1, high, total - high))
        out[rows, width:] = extra.astype(BF16)


def expert_kernel(rows, w_in, w_out, out):
    hidden = w_in.shape[1]
    step = 768
    x = rows[...]
    acc = jnp.zeros(out.shape, F32)
    for start in range(0, hidden, step):
        part = slice(start, start + step)
        h = jax.nn.gelu(dot(x, w_in[:, part]), approximate=True).astype(BF16)
        acc = acc + dot(h, w_out[part, :])
    out[...] = acc.astype(BF16)


def unpack(rows, width):
    sums = rows[..., :width].astype(F32)
    extra = rows[..., width : width + 3].astype(F32)
    return sums, extra[..., 0], extra[..., 1] + extra[..., 2]


def per_device(tokens, slot_query, expert_in, expert_out):
    x = tokens[0]
    count, width = x.shape
    chips = lax.axis_size("x") * lax.axis_size("y")
    grp_count = lax.axis_size("grp")
    slots = slot_query.shape[1]
    half = slots // 2
    slot_rows = half // chips
    x2 = lax.ppermute(x, "core", SWAP)

    core = lax.axis_index("core")
    split = slot_query.T.reshape(chips, 2, slot_rows, width)
    own_q = jnp.where(core == 0, split[:, 0], split[:, 1]).reshape(half, width)
    other_q = jnp.where(core == 0, split[:, 1], split[:, 0]).reshape(half, width)
    own_logits, own_w, other_w = call(
        row_kernel,
        [
            jax.ShapeDtypeStruct((half, count), F32),
            jax.ShapeDtypeStruct((half, count), BF16),
            jax.ShapeDtypeStruct((half, count), BF16),
        ],
        2 * slots * width * count, 5_000_000, own_q, other_q, x,
    )
    (packed,) = call(
        column_kernel,
        [jax.ShapeDtypeStruct((half, width + EXTRA), BF16)],
        3 * slots * width * count, 5_000_000, own_q, own_logits, x, x2,
    )
    parts = lax.all_to_all(
        packed.reshape(chips, slot_rows, -1), ("x", "y"), split_axis=0, concat_axis=0, tiled=True
    )
    sums, peak, total = unpack(parts, width)
    weight = jnp.exp(peak - jnp.max(peak, axis=0))
    slot_inputs = (
        jnp.sum(sums * weight[..., None], axis=0) / jnp.sum(total * weight, axis=0)[:, None]
    ).astype(BF16)

    received = lax.all_to_all(
        slot_inputs.reshape(grp_count, slot_rows // grp_count, width),
        "grp", split_axis=0, concat_axis=0, tiled=True,
    )
    (produced,) = call(
        expert_kernel,
        [jax.ShapeDtypeStruct((slot_rows, width), BF16)],
        4 * slot_rows * width * expert_in.shape[2], 9_500_000,
        received.reshape(slot_rows, width),
        pltpu.with_memory_space_constraint(expert_in[0], pltpu.VMEM),
        pltpu.with_memory_space_constraint(expert_out[0], pltpu.VMEM),
    )
    returned = lax.all_to_all(
        produced.reshape(received.shape), "grp", split_axis=0, concat_axis=0, tiled=True
    ).reshape(1, slot_rows, width)
    own = lax.all_to_all(
        jnp.broadcast_to(returned, (chips, slot_rows, width)),
        ("x", "y"), split_axis=0, concat_axis=0, tiled=True,
    ).reshape(half, width)
    other = lax.ppermute(own, "core", SWAP)
    over_slots = (((0,), (0,)), ((), ()))
    mixed = dot(own_w, own, over_slots)
    mixed = mixed + dot(other_w, other, over_slots)
    return mixed.astype(BF16)[None]


def solution(mesh):
    fine = Mesh(mesh.devices.reshape(4, 4, 2, 8), ("x", "y", "core", "grp"))
    ctx = ("x", "y", "core")
    in_specs = (
        P("grp", ctx, None),
        P(),
        P(ctx + ("grp",), None, None),
        P(ctx + ("grp",), None, None),
    )
    return jax.shard_map(
        per_device, mesh=fine, in_specs=in_specs, out_specs=P("grp", ctx, None), check_vma=False
    )
```

time: 87.6 us -> 87.5 us (level)
  matrix products: 11.7 us -> 2.38 us
  Pallas kernels: 0 us -> 7.38 us
  local copies, waits for them, and re-layouts: 3.52 us -> 7.81 us
  waiting for transfers between devices: 3.28 us -> 1.21 us
    dot_general x7 -> x2, matrix products: 11.7 us -> 2.38 us  [dot(): return lax.dot_general(a, b, dims, preferred_element_type=F32)]
    pallas_call x0 -> x3, Pallas kernels: none -> 7.38 us  [call(): pl.pallas_call(body, out_shape=outs, in_specs=[pl.BlockSpec(memory_space=...]
    unnamed x8, local copies, waits for them, and re-layouts: 1.97 us -> 7.54 us
    ppermute x1, waiting for transfers between devices: 2.1 us -> 0.01 us  [per_device(): x2 = lax.ppermute(x, 'core', SWAP)]
    select_n x1, other arithmetic: 0.11 us -> 1.56 us  [per_device(): jnp.where(core == 0, split[:, 1], split[:, 0]).reshape(half, width)]
    concatenate x1 -> x0, local copies, waits for them, and re-layouts: 1.28 us -> none  [pack(): return jnp.concatenate([sums.astype(BF16), extra.astype(BF16)], axis=1)]
    reduce_sum x1 -> x0, other arithmetic: 1.25 us -> none  [per_device(): row_total = jnp.sum(own_weights, axis=1) + jnp.sum(other_weights, axis=1)]
  transfers between devices with their start and end apart: 2 -> 2, of which waited for: 2 -> 1; matrix products, arithmetic and copies ran while one was open for 1% -> 6% of each run, Pallas kernels for 0% -> 2%
where the time goes in v2:
time: 87.5 us; the launch traced here: 87.2 us
  blocking collectives  58 us (66%)
  starting transfers between devices  8.3 us (9%)
  local copies, waits for them, and re-layouts  7.81 us (9%)
  Pallas kernels  7.38 us (8%)
  matrix products  2.38 us (3%)
  other arithmetic  1.95 us (2%)
  waiting for transfers between devices  1.21 us (1%)
    all_to_all x1, blocking collectives, per_device(): lax.all_to_all(packed.reshape(chips, slot_rows, -1), ('x', 'y'), split_ax...  19.4 us
    all_to_all x1, blocking collectives, per_device(): lax.all_to_all(slot_inputs.reshape(grp_count, slot_rows // grp_count, wid...  15 us
    all_to_all x1, blocking collectives, per_device(): lax.all_to_all(jnp.broadcast_to(returned, (chips, slot_rows, width)), ('x...  14.2 us
    all_to_all x1, blocking collectives, per_device(): lax.all_to_all(produced.reshape(received.shape), 'grp', split_axis=0, con...  9.42 us
    unnamed x8, local copies, waits for them, and re-layouts  7.54 us
    pallas_call x3, Pallas kernels, call(): pl.pallas_call(body, out_shape=outs, in_specs=[pl.BlockSpec(memory_space=...  7.38 us
    ppermute x1, starting transfers between devices, per_device(): other = lax.ppermute(own, 'core', SWAP)  5.06 us
    ppermute x1, starting transfers between devices, per_device(): x2 = lax.ppermute(x, 'core', SWAP)  3.24 us
  transfers between devices with their start and end apart: 2, of which 1 were waited for; matrix products, arithmetic and copies ran while one was open for 6% of the time, Pallas kernels for 2%

profile of v2, /device:TPU:1, one launch (start us, length us, event | category | flops | bytes accessed | tf_op | source)
XLA Modules:
  0.0 87.2 jit_solution(1567845168918272336)
XLA Ops:
  0.0 3.2 %collective-permute-start = (bf16[640,768]{1,0:T(8,128)(2,1)}, bf16[640,768]{1,0:T(8,128)(2,1)S(1)}, u32[]{:S(2)}, u32[]{:S(2)}) collective-permute-start(bf16[640,768]{1,0:T(8,128)(2,1)} %bitcast.36), channel_id=1, source_target_pairs={{0,8},{8,0},{1,9},{9,1},{2,10},{10,2},{3,11},{11,3},{4,12},{12,4},... | collective-permute-start | bytes 2949128 | tf_op jit(solution)/shard_map/ppermute | solution.py:93
  3.2 2.6 %copy.14 = bf16[768,1024]{0,1:T(8,128)(2,1)} copy(bf16[768,1024]{1,0:T(8,128)(2,1)} %param.5) | data formatting | bytes 3145728 | tf_op args[1]
  5.8 0.0 copy-start.2
  5.8 1.6 %broadcast_select_fusion = (bf16[16,1,32,768]{3,2,1,0:T(8,128)(2,1)S(1)}, bf16[16,1,32,768]{3,2,1,0:T(8,128)(2,1)S(1)}) fusion(pred[]{:T(512)S(6)} %eq.4, bf16[16,2,32,768]{3,2,1,0:T(8,128)(2,1)} %bitcast.39), kind=kLoop, calls=%fused_computation.3 | loop fusion | flops 786432 | bytes 3145729 | tf_op jit(solution)/shard_map/jit(_where)/select_n | solution.py:98
  7.4 0.1 copy-done.2
  7.5 1.9 %shard_map.46 = (f32[512,640]{1,0:T(8,128)S(1)}, bf16[512,640]{1,0:T(8,128)(2,1)S(1)}, bf16[512,640]{1,0:T(8,128)(2,1)S(1)}) custom-call(bf16[512,768]{1,0:T(8,128)(2,1)S(1)} %bitcast.33, bf16[512,768]{1,0:T(8,128)(2,1)S(1)} %bitcast.35, bf16[640,768]{1,0:T(8,128)(2,1)S(1)} %bitcast.37), custom_call_target="tpu_custom_call" | custom-call | flops 1006632960 | bytes 5000000 | tf_op jit(solution)/shard_map/pallas_call | solution.py:21
  9.4 0.0 collective-permute-done.x2
  9.4 3.6 %shard_map.47 = bf16[512,896]{1,0:T(8,128)(2,1)S(1)} custom-call(bf16[512,768]{1,0:T(8,128)(2,1)S(1)} %bitcast.34, f32[512,640]{1,0:T(8,128)S(1)} %get-tuple-element.9.logits, bf16[640,768]{1,0:T(8,128)(2,1)S(1)} %bitcast.38, bf16[640,768]{1,0:T(8,128)(2,1)S(1)} %collective-permute-done.x2), custom_call_target="tpu_custom_call" | custom-call | flops 1509949440 | bytes 5000000 | tf_op jit(solution)/shard_map/pallas_call | solution.py:21
  13.0 19.4 %all_to_all.20 = bf16[16,32,896]{2,1,0:T(8,128)(2,1)S(1)} all-to-all(bf16[16,32,896]{2,1,0:T(8,128)(2,1)S(1)} %bitcast.32), channel_id=1, replica_groups=mesh['x'=4,'y'=4,'core'=2,'grp'=8] {'x','y'}, dimensions={0} | all-to-all | bytes 1835008 | tf_op jit(solution)/shard_map/all_to_all | solution.py:113
  32.5 0.2 copy.19
  32.7 0.2 multiply_reduce_fusion
  33.0 0.1 div.11
  33.1 0.1 divide_convert_fusion
  33.2 15.0 %all_to_all.21 = bf16[8,4,768]{2,1,0:T(4,128)(2,1)S(1)} all-to-all(bf16[8,4,768]{2,1,0:T(4,128)(2,1)S(1)} %divide_convert_fusion), channel_id=1, replica_groups=mesh['x'=4,'y'=4,'core'=2,'grp'=8] {'grp'}, dimensions={0} | all-to-all | bytes 98304 | tf_op jit(solution)/shard_map/all_to_all | solution.py:122
  48.2 0.0 copy-start
  48.2 2.3 %copy-done = bf16[1,768,3072]{2,1,0:T(8,128)(2,1)S(1)} copy-done((bf16[1,768,3072]{2,1,0:T(8,128)(2,1)S(1)}, bf16[1,768,3072]{2,1,0:T(8,128)(2,1)}, u32[]{:S(2)}) %copy-start) | copy-done | bytes 4718616
  50.5 0.0 copy-start.1
  50.6 2.3 %copy-done.1 = bf16[1,3072,768]{2,1,0:T(8,128)(2,1)S(1)} copy-done((bf16[1,3072,768]{2,1,0:T(8,128)(2,1)S(1)}, bf16[1,3072,768]{2,1,0:T(8,128)(2,1)}, u32[]{:S(2)}) %copy-start.1) | copy-done | bytes 4718616
  52.9 1.9 %shard_map.48 = bf16[32,768]{1,0:T(8,128)(2,1)S(1)} custom-call(bf16[32,768]{1,0:T(8,128)(2,1)S(1)} %reshape.44.rows, bf16[768,3072]{1,0:T(8,128)(2,1)S(1)} %bitcast.30, bf16[3072,768]{1,0:T(8,128)(2,1)S(1)} %bitcast.31), custom_call_target="tpu_custom_call" | custom-call | flops 301989888 | bytes 9500000 | tf_op jit(solution)/shard_map/pallas_call | solution.py:21
  54.8 9.4 %all_to_all.22 = bf16[8,4,768]{2,1,0:T(4,128)(2,1)S(1)} all-to-all(bf16[8,4,768]{2,1,0:T(4,128)(2,1)S(1)} %reshape.45), channel_id=1, replica_groups=mesh['x'=4,'y'=4,'core'=2,'grp'=8] {'grp'}, dimensions={0} | all-to-all | bytes 98304 | tf_op jit(solution)/shard_map/all_to_all | solution.py:134
  64.2 0.1 broadcast_in_dim.14
  64.3 14.2 %all_to_all.23 = bf16[16,32,768]{2,1,0:T(8,128)(2,1)S(1)} all-to-all(bf16[16,32,768]{2,1,0:T(8,128)(2,1)S(1)} %broadcast_in_dim.14), channel_id=1, replica_groups=mesh['x'=4,'y'=4,'core'=2,'grp'=8] {'x','y'}, dimensions={0} | all-to-all | bytes 1572864 | tf_op jit(solution)/shard_map/all_to_all | solution.py:137
  78.5 5.1 %collective-permute-start.1 = (bf16[512,768]{1,0:T(8,128)(2,1)S(1)}, bf16[512,768]{1,0:T(8,128)(2,1)S(1)}, u32[]{:S(2)}, u32[]{:S(2)}) collective-permute-start(bf16[512,768]{1,0:T(8,128)(2,1)S(1)} %bitcast.40), channel_id=1, source_target_pairs={{0,8},{8,0},{1,9},{9,1},{2,10},{10,2},{3,11},{11,3},{4,12},{12,4},... | collective-permute-start | bytes 2359304 | tf_op jit(solution)/shard_map/ppermute | solution.py:141
  83.6 0.7 fusion.5
  84.3 1.2 %collective-permute-done.1 = bf16[512,768]{1,0:T(8,128)(2,1)S(1)} collective-permute-done((bf16[512,768]{1,0:T(8,128)(2,1)S(1)}, bf16[512,768]{1,0:T(8,128)(2,1)S(1)}, u32[]{:S(2)}, u32[]{:S(2)}) %collective-permute-start.1) | collective-permute-done | bytes 786464 | tf_op jit(solution)/shard_map/ppermute | solution.py:141
  85.5 1.7 %fusion = bf16[1,640,768]{2,1,0:T(8,128)(2,1)} fusion(f32[640,768]{1,0:T(8,128)S(1)} %fusion.5, bf16[512,640]{1,0:T(8,128)(2,1)S(1)} %get-tuple-element.10, bf16[512,768]{1,0:T(8,128)(2,1)S(1)} %collective-permute-done.1), kind=kOutput, calls=%fused_computation.2 | convolution fusion | flops 504299520 | bytes 4390912 | tf_op jit(solution)/shard_map/dot_general | solution.py:17
  (9 shorter events, 0.2 us)
Async XLA Ops:
  0.0 9.4 %collective-permute-start = (bf16[640,768]{1,0:T(8,128)(2,1)}, bf16[640,768]{1,0:T(8,128)(2,1)S(1)}, u32[]{:S(2)}, u32[]{:S(2)}) collective-permute-start(bf16[640,768]{1,0:T(8,128)(2,1)} %bitcast.36), channel_id=1, source_target_pairs={{0,8},{8,0},{1,9},{9,1},{2,10},{10,2},{3,11},{11,3},{4,12},{12,4},... | collective-permute-start | bytes 2949128 | tf_op jit(solution)/shard_map/ppermute | solution.py:93
  5.8 1.7 %copy-start.2 = (bf16[1,640,768]{2,1,0:T(8,128)(2,1)S(1)}, bf16[1,640,768]{2,1,0:T(8,128)(2,1)}, u32[]{:S(2)}) copy-start(bf16[1,640,768]{2,1,0:T(8,128)(2,1)} %param.4) | copy-start | bytes 2949124
  48.2 2.3 %copy-start = (bf16[1,768,3072]{2,1,0:T(8,128)(2,1)S(1)}, bf16[1,768,3072]{2,1,0:T(8,128)(2,1)}, u32[]{:S(2)}) copy-start(bf16[1,768,3072]{2,1,0:T(8,128)(2,1)} %param.6) | copy-start | bytes 14155780
  50.5 2.3 %copy-start.1 = (bf16[1,3072,768]{2,1,0:T(8,128)(2,1)S(1)}, bf16[1,3072,768]{2,1,0:T(8,128)(2,1)}, u32[]{:S(2)}) copy-start(bf16[1,3072,768]{2,1,0:T(8,128)(2,1)} %param.7) | copy-start | bytes 14155780
  78.5 7.0 %collective-permute-start.1 = (bf16[512,768]{1,0:T(8,128)(2,1)S(1)}, bf16[512,768]{1,0:T(8,128)(2,1)S(1)}, u32[]{:S(2)}, u32[]{:S(2)}) collective-permute-start(bf16[512,768]{1,0:T(8,128)(2,1)S(1)} %bitcast.40), channel_id=1, source_target_pairs={{0,8},{8,0},{1,9},{9,1},{2,10},{10,2},{3,11},{11,3},{4,12},{12,4},... | collective-permute-start | bytes 2359304 | tf_op jit(solution)/shard_map/ppermute | solution.py:141

commit v3 on v2

v3 whole, which is shorter than its diff:
```python
import functools

import jax
import jax.numpy as jnp
from jax import lax
from jax.experimental import pallas as pl
from jax.experimental.pallas import tpu as pltpu
from jax.sharding import Mesh, PartitionSpec as P

BF16 = jnp.bfloat16
F32 = jnp.float32
SWAP = [(0, 1), (1, 0)]
LIMIT = 24 * 1024 * 1024
FRONT = LIMIT
BLOCK = 512
EXTRA = 128
TRANSPOSED = (((1,), (1,)), ((), ()))


def dot(a, b, dims=(((1,), (0,)), ((), ()))):
    return lax.dot_general(a, b, dims, preferred_element_type=F32)


def call(body, outs, flops, moved, args, scratch=(), space=pltpu.VMEM, limit=LIMIT):
    return pl.pallas_call(
        body,
        out_shape=outs,
        in_specs=[pl.BlockSpec(memory_space=space)] * len(args),
        out_specs=[pl.BlockSpec(memory_space=pltpu.VMEM)] * len(outs),
        scratch_shapes=list(scratch),
        compiler_params=pltpu.CompilerParams(vmem_limit_bytes=limit),
        cost_estimate=pl.CostEstimate(flops=flops, bytes_accessed=moved, transcendentals=0),
    )(*args)


def peak_of(logits):
    return jnp.max(logits, axis=1, keepdims=True).astype(BF16).astype(F32)


def row_kernel(slot_rows, q_hbm, x_hbm, own_q, own_logits, other_logits, sums, stats, q, x, other_q, sems):
    group = 256
    kept = group // 2
    blocks = q.shape[1] // group
    loads = []
    for b in range(blocks):
        columns = slice(b * group, (b + 1) * group)
        loads.append(
            pltpu.make_async_copy(q_hbm.at[:, columns], q.at[:, columns], sems.at[b])
        )
    loads.append(pltpu.make_async_copy(x_hbm, x, sems.at[blocks]))
    for load in loads:
        load.start()
    core = lax.axis_index("core")
    pair = 2 * slot_rows
    row = lax.broadcasted_iota(jnp.int32, (group, group), 0)
    column = lax.broadcasted_iota(jnp.int32, (group, group), 1)
    kind = row // kept
    row = row % kept
    place = row // slot_rows * pair + row % slot_rows + (kind ^ core) * slot_rows
    pick = jnp.where(column == place, 1.0, 0.0).astype(BF16)
    for b in range(blocks):
        loads[b].wait()
        picked = dot(pick, q[:, b * group : (b + 1) * group], TRANSPOSED).astype(BF16)
        rows = slice(b * kept, (b + 1) * kept)
        own_q[rows, :] = picked[:kept]
        other_q[rows, :] = picked[kept:]
    loads[blocks].wait()
    tokens = x[...]
    own = [dot(own_q[rows, :], tokens, TRANSPOSED) for rows in halves(own_q)]
    lane = lax.broadcasted_iota(jnp.int32, (BLOCK, EXTRA), 1)
    for rows, logits in zip(halves(own_q), own):
        own_logits[rows, :] = logits
        top = peak_of(logits)
        scaled = jnp.exp(logits - top)
        total = jnp.sum(scaled, axis=1, keepdims=True)
        sums[rows, :] = dot(scaled.astype(BF16), tokens)
        stats[rows, :] = jnp.where(lane == 0, top, total)
        other_logits[rows, :] = dot(other_q[rows, :], tokens, TRANSPOSED)


def halves(ref):
    return [slice(start, start + BLOCK) for start in range(0, ref.shape[0], BLOCK)]


def softmax_kernel(own_logits, other_logits, own_w, other_w):
    own, other = own_logits[...], other_logits[...]
    top = jnp.maximum(jnp.max(own, axis=0, keepdims=True), jnp.max(other, axis=0, keepdims=True))
    own = jnp.exp(own - top)
    other = jnp.exp(other - top)
    total = jnp.sum(own, axis=0, keepdims=True) + jnp.sum(other, axis=0, keepdims=True)
    scale = 1.0 / total
    own_w[...] = (own * scale).astype(BF16)
    other_w[...] = (other * scale).astype(BF16)


def column_kernel(own_q, x2, sums, stats, out):
    width = own_q.shape[1]
    tokens = x2[...]
    lane = lax.broadcasted_iota(jnp.int32, (BLOCK, EXTRA), 1)
    parts = [dot(own_q[rows, :], tokens, TRANSPOSED) for rows in halves(own_q)]
    for rows, logits in zip(halves(own_q), parts):
        top2 = peak_of(logits)
        scaled = jnp.exp(logits - top2)
        top1, total1 = stats[rows, 0:1], stats[rows, 1:2]
        top = jnp.maximum(top1, top2)
        w1, w2 = jnp.exp(top1 - top), jnp.exp(top2 - top)
        total = total1 * w1 + jnp.sum(scaled, axis=1, keepdims=True) * w2
        both = sums[rows, :] * w1 + dot(scaled.astype(BF16), tokens) * w2
        out[rows, :width] = both.astype(BF16)
        high = total.astype(BF16).astype(F32)
        extra = jnp.where(lane == 0, top, jnp.where(lane == 1, high, total - high))
        out[rows, width:] = extra.astype(BF16)


def combine_kernel(parts, out, scratch):
    chips = parts.shape[0]
    groups, held, width = out.shape
    extra = [parts[c, :, width:].astype(F32) for c in range(chips)]
    top = extra[0][:, 0:1]
    for c in range(1, chips):
        top = jnp.maximum(top, extra[c][:, 0:1])
    total = jnp.zeros(top.shape, F32)
    acc = jnp.zeros(scratch.shape, F32)
    for c in range(chips):
        weight = jnp.exp(extra[c][:, 0:1] - top)
        total = total + weight * (extra[c][:, 1:2] + extra[c][:, 2:3])
        acc = acc + weight * parts[c, :, :width].astype(F32)
    scratch[...] = acc / total
    for g in range(groups):
        out[g] = scratch[g * held : (g + 1) * held, :].astype(BF16)


def expert_kernel(received, w_in, w_out, out, scratch):
    groups, held, _ = received.shape
    for g in range(groups):
        scratch[g * held : (g + 1) * held, :] = received[g].astype(F32)
    x = scratch[...].astype(BF16)
    hidden = w_in.shape[1]
    step = 768
    acc = jnp.zeros(scratch.shape, F32)
    for start in range(0, hidden, step):
        part = slice(start, start + step)
        h = jax.nn.gelu(dot(x, w_in[:, part]), approximate=True).astype(BF16)
        acc = acc + dot(h, w_out[part, :])
    scratch[...] = acc
    for g in range(groups):
        out[g] = scratch[g * held : (g + 1) * held, :].astype(BF16)


def per_device(tokens, slot_query, expert_in, expert_out):
    x = tokens[0]
    count, width = x.shape
    chips = lax.axis_size("x") * lax.axis_size("y")
    grp_count = lax.axis_size("grp")
    slots = slot_query.shape[1]
    half = slots // 2
    slot_rows = half // chips
    x2 = lax.ppermute(x, "core", SWAP)
    shape = jax.ShapeDtypeStruct
    own_q, own_logits, other_logits, sums, stats = call(
        functools.partial(row_kernel, slot_rows),
        [
            shape((half, width), BF16),
            shape((half, count), F32),
            shape((half, count), F32),
            shape((half, width), F32),
            shape((half, EXTRA), F32),
        ],
        3 * slots * width * count, 5_000_000,
        [pltpu.with_memory_space_constraint(a, pltpu.HBM) for a in (slot_query, x)],
        [
            pltpu.VMEM((width, slots), BF16),
            pltpu.VMEM((count, width), BF16),
            pltpu.VMEM((half, width), BF16),
            pltpu.SemaphoreType.DMA((5,)),
        ],
        pl.ANY,
        FRONT,
    )
    (packed,) = call(
        column_kernel,
        [shape((half, width + EXTRA), BF16)],
        2 * slots * width * count, 5_000_000, (own_q, x2, sums, stats), limit=FRONT,
    )
    w_in, w_out = expert_in[0], expert_out[0]
    parts = lax.all_to_all(
        packed.reshape(chips, slot_rows, -1), ("x", "y"), split_axis=0, concat_axis=0, tiled=True
    )
    block = shape((grp_count, slot_rows // grp_count, width), BF16)
    rows = [pltpu.VMEM((slot_rows, width), F32)]
    (slot_inputs,) = call(combine_kernel, [block], 2 * half * width, 1_000_000, (parts,), rows)
    received = lax.all_to_all(slot_inputs, "grp", split_axis=0, concat_axis=0, tiled=True)
    (produced,) = call(
        expert_kernel,
        [block],
        4 * slot_rows * width * expert_in.shape[2], 9_500_000,
        (
            received,
            pltpu.with_memory_space_constraint(w_in, pltpu.VMEM),
            pltpu.with_memory_space_constraint(w_out, pltpu.VMEM),
        ),
        rows,
    )
    returned = lax.all_to_all(
        produced, "grp", split_axis=0, concat_axis=0, tiled=True
    ).reshape(1, slot_rows, width)
    own = lax.all_to_all(
        jnp.broadcast_to(returned, (chips, slot_rows, width)),
        ("x", "y"), split_axis=0, concat_axis=0, tiled=True,
    ).reshape(half, width)
    other = lax.ppermute(own, "core", SWAP)
    own_w, other_w = call(
        softmax_kernel,
        [shape((half, count), BF16), shape((half, count), BF16)],
        10 * slots * count, 4_000_000, (own_logits, other_logits),
    )
    over_slots = (((0,), (0,)), ((), ()))
    mixed = dot(own_w, own, over_slots)
    mixed = mixed + dot(other_w, other, over_slots)
    return mixed.astype(BF16)[None]


def solution(mesh):
    fine = Mesh(mesh.devices.reshape(4, 4, 2, 8), ("x", "y", "core", "grp"))
    ctx = ("x", "y", "core")
    in_specs = (
        P("grp", ctx, None),
        P(),
        P(ctx + ("grp",), None, None),
        P(ctx + ("grp",), None, None),
    )
    return jax.shard_map(
        per_device, mesh=fine, in_specs=in_specs, out_specs=P("grp", ctx, None), check_vma=False
    )
```

time: 87.5 us -> 80 us (0.914)
  local copies, waits for them, and re-layouts: 7.81 us -> 0.1 us
  Pallas kernels: 7.38 us -> 10.5 us
  other arithmetic: 1.95 us -> 0 us
    unnamed x8 -> x4, local copies, waits for them, and re-layouts: 7.54 us -> 0.01 us
    pallas_call x3 -> x5, Pallas kernels: 7.38 us -> 10.5 us  [call(): pl.pallas_call(body, out_shape=outs, in_specs=[pl.BlockSpec(memory_space=...]
    select_n x1 -> x0, other arithmetic: 1.56 us -> none  [per_device(): jnp.where(core == 0, split[:, 1], split[:, 0]).reshape(half, width)]
  transfers between devices with their start and end apart: 2 -> 2, of which waited for: 1 -> 1; matrix products, arithmetic and copies ran while one was open for 6% -> 1% of each run, Pallas kernels for 2% -> 7%
where the time goes in v3:
time: 80 us; the launch traced here: 79.7 us
  blocking collectives  58 us (72%)
  Pallas kernels  10.5 us (13%)
  starting transfers between devices  8.3 us (10%)
  matrix products  2.37 us (3%)
    all_to_all x1, blocking collectives, per_device(): lax.all_to_all(packed.reshape(chips, slot_rows, -1), ('x', 'y'), split_ax...  19.4 us
    all_to_all x1, blocking collectives, per_device(): lax.all_to_all(slot_inputs, 'grp', split_axis=0, concat_axis=0, tiled=True)  15.1 us
    all_to_all x1, blocking collectives, per_device(): lax.all_to_all(jnp.broadcast_to(returned, (chips, slot_rows, width)), ('x...  14.2 us
    pallas_call x5, Pallas kernels, call(): pl.pallas_call(body, out_shape=outs, in_specs=[pl.BlockSpec(memory_space=...  10.5 us
    all_to_all x1, blocking collectives, per_device(): lax.all_to_all(produced, 'grp', split_axis=0, concat_axis=0, tiled=True)  9.42 us
    ppermute x1, starting transfers between devices, per_device(): other = lax.ppermute(own, 'core', SWAP)  5.06 us
    ppermute x1, starting transfers between devices, per_device(): x2 = lax.ppermute(x, 'core', SWAP)  3.24 us
    dot_general x2, matrix products, dot(): return lax.dot_general(a, b, dims, preferred_element_type=F32)  2.37 us
  transfers between devices with their start and end apart: 2, of which 1 were waited for; matrix products, arithmetic and copies ran while one was open for 1% of the time, Pallas kernels for 7%

profile of v3, /device:TPU:1, one launch (start us, length us, event | category | flops | bytes accessed | tf_op | source)
XLA Modules:
  0.0 79.7 jit_solution(14709063005142665634)
XLA Ops:
  0.0 3.2 %collective-permute-start = (bf16[640,768]{1,0:T(8,128)(2,1)}, bf16[640,768]{1,0:T(8,128)(2,1)S(1)}, u32[]{:S(2)}, u32[]{:S(2)}) collective-permute-start(bf16[640,768]{1,0:T(8,128)(2,1)} %bitcast.16), channel_id=1, source_target_pairs={{0,8},{8,0},{1,9},{9,1},{2,10},{10,2},{3,11},{11,3},{4,12},{12,4},... | collective-permute-start | bytes 2949128 | tf_op jit(solution)/shard_map/ppermute | solution.py:158
  3.2 0.0 copy-start.1
  3.2 4.8 %shard_map.46 = (bf16[512,768]{1,0:T(8,128)(2,1)S(1)}, f32[512,640]{1,0:T(8,128)S(1)}, f32[512,640]{1,0:T(8,128)S(1)}, f32[512,768]{1,0:T(8,128)S(1)}, f32[512,128]{1,0:T(8,128)S(1)}) custom-call(bf16[768,1024]{1,0:T(8,128)(2,1)} %q_hbm.1, bf16[640,768]{1,0:T(8,128)(2,1)} %bitcast.17), custom_call_target="tpu_custom_call" | custom-call | flops 1509949440 | bytes 5000000 | tf_op jit(solution)/shard_map/pallas_call | solution.py:25
  8.1 0.0 collective-permute-done.x2
  8.1 0.0 copy-start
  8.1 2.4 %shard_map.48 = bf16[512,896]{1,0:T(8,128)(2,1)S(1)} custom-call(bf16[512,768]{1,0:T(8,128)(2,1)S(1)} %get-tuple-element.15.own_q, bf16[640,768]{1,0:T(8,128)(2,1)S(1)} %collective-permute-done.x2, f32[512,768]{1,0:T(8,128)S(1)} %get-tuple-element.16.sums, f32[512,128]{1,0:T(8,128)S(1)} %get-tuple-element.17.stats), custom_call_target="tpu_custom_call" | custom-call | flops 1006632960 | bytes 5000000 | tf_op jit(solution)/shard_map/pallas_call | solution.py:25
  10.5 19.4 %all_to_all.20.parts = bf16[16,32,896]{2,1,0:T(8,128)(2,1)S(1)} all-to-all(bf16[16,32,896]{2,1,0:T(8,128)(2,1)S(1)} %bitcast.13), channel_id=1, replica_groups=mesh['x'=4,'y'=4,'core'=2,'grp'=8] {'x','y'}, dimensions={0} | all-to-all | bytes 1835008 | tf_op jit(solution)/shard_map/all_to_all | solution.py:186
  29.9 0.6 shard_map.49
  30.5 15.1 %all_to_all.21.received = bf16[8,4,768]{2,1,0:T(4,128)(2,1)S(1)} all-to-all(bf16[8,4,768]{2,1,0:T(4,128)(2,1)S(1)} %shard_map.49), channel_id=1, replica_groups=mesh['x'=4,'y'=4,'core'=2,'grp'=8] {'grp'}, dimensions={0} | all-to-all | bytes 98304 | tf_op jit(solution)/shard_map/all_to_all | solution.py:192
  45.5 0.0 copy-done.1
  45.5 0.0 copy-done
  45.5 1.9 %shard_map.50 = bf16[8,4,768]{2,1,0:T(4,128)(2,1)S(1)} custom-call(bf16[8,4,768]{2,1,0:T(4,128)(2,1)S(1)} %all_to_all.21.received, bf16[768,3072]{1,0:T(8,128)(2,1)S(1)} %bitcast.11, bf16[3072,768]{1,0:T(8,128)(2,1)S(1)} %bitcast.12), custom_call_target="tpu_custom_call" | custom-call | flops 301989888 | bytes 9500000 | tf_op jit(solution)/shard_map/pallas_call | solution.py:25
  47.4 9.4 %all_to_all.22 = bf16[8,4,768]{2,1,0:T(4,128)(2,1)S(1)} all-to-all(bf16[8,4,768]{2,1,0:T(4,128)(2,1)S(1)} %shard_map.50), channel_id=1, replica_groups=mesh['x'=4,'y'=4,'core'=2,'grp'=8] {'grp'}, dimensions={0} | all-to-all | bytes 98304 | tf_op jit(solution)/shard_map/all_to_all | solution.py:204
  56.8 0.1 broadcast_in_dim.11
  56.9 14.2 %all_to_all.23 = bf16[16,32,768]{2,1,0:T(8,128)(2,1)S(1)} all-to-all(bf16[16,32,768]{2,1,0:T(8,128)(2,1)S(1)} %broadcast_in_dim.11), channel_id=1, replica_groups=mesh['x'=4,'y'=4,'core'=2,'grp'=8] {'x','y'}, dimensions={0} | all-to-all | bytes 1572864 | tf_op jit(solution)/shard_map/all_to_all | solution.py:207
  71.1 5.1 %collective-permute-start.1 = (bf16[512,768]{1,0:T(8,128)(2,1)S(1)}, bf16[512,768]{1,0:T(8,128)(2,1)S(1)}, u32[]{:S(2)}, u32[]{:S(2)}) collective-permute-start(bf16[512,768]{1,0:T(8,128)(2,1)S(1)} %bitcast.14), channel_id=1, source_target_pairs={{0,8},{8,0},{1,9},{9,1},{2,10},{10,2},{3,11},{11,3},{4,12},{12,4},... | collective-permute-start | bytes 2359304 | tf_op jit(solution)/shard_map/ppermute | solution.py:211
  76.2 0.8 shard_map.47
  76.9 0.7 fusion.1
  77.6 0.4 collective-permute-done.1
  78.1 1.7 %fusion = bf16[1,640,768]{2,1,0:T(8,128)(2,1)} fusion(f32[640,768]{1,0:T(8,128)S(1)} %fusion.1, bf16[512,640]{1,0:T(8,128)(2,1)S(1)} %get-tuple-element.18, bf16[512,768]{1,0:T(8,128)(2,1)S(1)} %collective-permute-done.1), kind=kOutput, calls=%fused_computation.1 | convolution fusion | flops 504299520 | bytes 4390912 | tf_op jit(solution)/shard_map/dot_general | solution.py:21
  (1 shorter events, 0.0 us)
Async XLA Ops:
  0.0 8.1 %collective-permute-start = (bf16[640,768]{1,0:T(8,128)(2,1)}, bf16[640,768]{1,0:T(8,128)(2,1)S(1)}, u32[]{:S(2)}, u32[]{:S(2)}) collective-permute-start(bf16[640,768]{1,0:T(8,128)(2,1)} %bitcast.16), channel_id=1, source_target_pairs={{0,8},{8,0},{1,9},{9,1},{2,10},{10,2},{3,11},{11,3},{4,12},{12,4},... | collective-permute-start | bytes 2949128 | tf_op jit(solution)/shard_map/ppermute | solution.py:158
  3.2 42.3 %copy-start.1 = (bf16[1,3072,768]{2,1,0:T(8,128)(2,1)S(1)}, bf16[1,3072,768]{2,1,0:T(8,128)(2,1)}, u32[]{:S(2)}) copy-start(bf16[1,3072,768]{2,1,0:T(8,128)(2,1)} %param.7) | copy-start | bytes 14155780
  8.1 37.5 %copy-start = (bf16[1,768,3072]{2,1,0:T(8,128)(2,1)S(1)}, bf16[1,768,3072]{2,1,0:T(8,128)(2,1)}, u32[]{:S(2)}) copy-start(bf16[1,768,3072]{2,1,0:T(8,128)(2,1)} %param.6) | copy-start | bytes 14155780
  71.1 7.0 %collective-permute-start.1 = (bf16[512,768]{1,0:T(8,128)(2,1)S(1)}, bf16[512,768]{1,0:T(8,128)(2,1)S(1)}, u32[]{:S(2)}, u32[]{:S(2)}) collective-permute-start(bf16[512,768]{1,0:T(8,128)(2,1)S(1)} %bitcast.14), channel_id=1, source_target_pairs={{0,8},{8,0},{1,9},{9,1},{2,10},{10,2},{3,11},{11,3},{4,12},{12,4},... | collective-permute-start | bytes 2359304 | tf_op jit(solution)/shard_map/ppermute | solution.py:211

commit v4 on v3

v4 whole, which is shorter than its diff:
```python
import functools

import jax
import jax.numpy as jnp
from jax import lax
from jax.experimental import pallas as pl
from jax.experimental.pallas import tpu as pltpu
from jax.sharding import Mesh, PartitionSpec as P

BF16 = jnp.bfloat16
F32 = jnp.float32
SWAP = [(0, 1), (1, 0)]
LIMIT = 24 * 1024 * 1024
LANES = 128
TAIL = 16
OVER_ROWS = (((0,), (0,)), ((), ()))


def dot(a, b, dims=(((1,), (0,)), ((), ()))):
    return lax.dot_general(a, b, dims, preferred_element_type=F32)


def call(body, outs, flops, moved, args, scratch=(), space=pltpu.VMEM):
    return pl.pallas_call(
        body,
        out_shape=outs,
        in_specs=[pl.BlockSpec(memory_space=space)] * len(args),
        out_specs=[pl.BlockSpec(memory_space=pltpu.VMEM)] * len(outs),
        scratch_shapes=list(scratch),
        compiler_params=pltpu.CompilerParams(vmem_limit_bytes=LIMIT),
        cost_estimate=pl.CostEstimate(flops=flops, bytes_accessed=moved, transcendentals=0),
    )(*args)


def peak_of(logits):
    return jnp.max(logits, axis=0, keepdims=True).astype(BF16).astype(F32)


def logit_kernel(slot_rows, q_hbm, x_hbm, own_q, other_q, x, logits, q, sems):
    group = 256
    kept = group // 2
    blocks = q.shape[1] // group
    loads = []
    for b in range(blocks):
        columns = slice(b * group, (b + 1) * group)
        loads.append(
            pltpu.make_async_copy(q_hbm.at[:, columns], q.at[:, columns], sems.at[b])
        )
    loads.append(pltpu.make_async_copy(x_hbm, x, sems.at[blocks]))
    for load in loads:
        load.start()
    core = lax.axis_index("core")
    pair = 2 * slot_rows
    row = lax.broadcasted_iota(jnp.int32, (group, group), 0)
    column = lax.broadcasted_iota(jnp.int32, (group, group), 1)
    kind = column // kept
    column = column % kept
    place = column // slot_rows * pair + column % slot_rows + (kind ^ core) * slot_rows
    pick = jnp.where(row == place, 1.0, 0.0).astype(BF16)
    for b in range(blocks):
        loads[b].wait()
        picked = dot(q[:, b * group : (b + 1) * group], pick).astype(BF16)
        columns = slice(b * kept, (b + 1) * kept)
        own_q[:, columns] = picked[:, :kept]
        other_q[:, columns] = picked[:, kept:]
    loads[blocks].wait()
    logits[...] = dot(x[...], own_q[...])


def column_kernel(own_q, x, x2, logits, out):
    width = own_q.shape[0]
    second = dot(x2[...], own_q[...])
    first = logits[...]
    top1 = peak_of(first)
    first = jnp.exp(first - top1)
    total1 = jnp.sum(first, axis=0, keepdims=True)
    sums1 = dot(first.astype(BF16), x[...], OVER_ROWS)
    top2 = peak_of(second)
    second = jnp.exp(second - top2)
    total2 = jnp.sum(second, axis=0, keepdims=True)
    sums2 = dot(second.astype(BF16), x2[...], OVER_ROWS)
    top = jnp.maximum(top1, top2)
    w1, w2 = jnp.exp(top1 - top), jnp.exp(top2 - top)
    total = total1 * w1 + total2 * w2
    high = total.astype(BF16).astype(F32)
    kind = lax.broadcasted_iota(jnp.int32, (LANES, top.shape[1]), 0)
    stats = total - high
    for place, value in enumerate((top, high, w1, w2)):
        stats = jnp.where(kind == place, value, stats)
    columns = stats.T
    sums = (sums1 * columns[:, 2:3] + sums2 * columns[:, 3:4]).astype(BF16)
    stats = stats[:TAIL].astype(BF16)
    chips, rows, _ = out.shape
    held = top.shape[1] // chips
    for c in range(chips):
        for j in range(width // LANES):
            part = slice(j * LANES, (j + 1) * LANES)
            out[c, j * held : (j + 1) * held, :] = sums[c * held : (c + 1) * held, part]
        group = c * held // LANES * LANES
        out[c, rows - TAIL :, :] = stats[:, group : group + LANES]


def softmax_kernel(x, other_q, logits, own_w, other_w):
    own = logits[...]
    other = dot(x[...], other_q[...])
    top = jnp.maximum(jnp.max(own, axis=1, keepdims=True), jnp.max(other, axis=1, keepdims=True))
    own = jnp.exp(own - top)
    other = jnp.exp(other - top)
    total = jnp.sum(own, axis=1, keepdims=True) + jnp.sum(other, axis=1, keepdims=True)
    scale = 1.0 / total
    own_w[...] = (own * scale).astype(BF16)
    other_w[...] = (other * scale).astype(BF16)


def combine_kernel(parts, out, weights, scratch):
    chips, rows, _ = parts.shape
    groups, size, width = out.shape
    held = groups * size
    source = lax.broadcasted_iota(jnp.int32, (LANES, LANES), 0)
    top = jnp.full((LANES, LANES), -jnp.inf, F32)
    total = jnp.zeros((LANES, LANES), F32)
    for c in range(chips):
        stats = parts[c, rows - TAIL :, :].astype(F32)
        top = jnp.where(source == c, stats[0:1], top)
        total = jnp.where(source == c, stats[1:2] + stats[4:5], total)
    weight = jnp.exp(top - jnp.max(top, axis=0, keepdims=True))
    weight = weight / jnp.sum(total * weight, axis=0, keepdims=True)
    weights[...] = weight.T
    chip = lax.axis_index("x") * lax.axis_size("y") + lax.axis_index("y")
    start = pl.multiple_of(chip % (LANES // held) * held, held)
    mine = weights[pl.ds(start, held), :]
    for j in range(width // LANES):
        part = slice(j * LANES, (j + 1) * LANES)
        acc = jnp.zeros((held, LANES), F32)
        for c in range(chips):
            acc = acc + mine[:, c : c + 1] * parts[c, j * held : (j + 1) * held, :].astype(F32)
        scratch[:, part] = acc
    for g in range(groups):
        out[g] = scratch[g * size : (g + 1) * size, :].astype(BF16)


def expert_kernel(received, w_in, w_out, out, scratch):
    groups, held, _ = received.shape
    for g in range(groups):
        scratch[g * held : (g + 1) * held, :] = received[g].astype(F32)
    x = scratch[...].astype(BF16)
    hidden = w_in.shape[1]
    step = 768
    acc = jnp.zeros(scratch.shape, F32)
    for start in range(0, hidden, step):
        part = slice(start, start + step)
        h = jax.nn.gelu(dot(x, w_in[:, part]), approximate=True).astype(BF16)
        acc = acc + dot(h, w_out[part, :])
    scratch[...] = acc
    for g in range(groups):
        out[g] = scratch[g * held : (g + 1) * held, :].astype(BF16)


def per_device(tokens, slot_query, expert_in, expert_out):
    x = tokens[0]
    count, width = x.shape
    chips = lax.axis_size("x") * lax.axis_size("y")
    grp_count = lax.axis_size("grp")
    slots = slot_query.shape[1]
    half = slots // 2
    slot_rows = half // chips
    x2 = lax.ppermute(x, "core", SWAP)
    shape = jax.ShapeDtypeStruct
    own_q, other_q, kept, logits = call(
        functools.partial(logit_kernel, slot_rows),
        [
            shape((width, half), BF16),
            shape((width, half), BF16),
            shape((count, width), BF16),
            shape((count, half), F32),
        ],
        2 * slots * width * count, 5_000_000,
        [pltpu.with_memory_space_constraint(a, pltpu.HBM) for a in (slot_query, x)],
        [pltpu.VMEM((width, slots), BF16), pltpu.SemaphoreType.DMA((5,))],
        pl.ANY,
    )
    (packed,) = call(
        column_kernel,
        [shape((chips, slot_rows * width // LANES + TAIL, LANES), BF16)],
        3 * slots * width * count, 5_000_000, (own_q, kept, x2, logits),
    )
    w_in, w_out = expert_in[0], expert_out[0]
    parts = lax.all_to_all(
        packed, ("x", "y"), split_axis=0, concat_axis=0, tiled=True
    )
    block = shape((grp_count, slot_rows // grp_count, width), BF16)
    rows = [pltpu.VMEM((slot_rows, width), F32)]
    (slot_inputs,) = call(
        combine_kernel, [block], 2 * half * width, 1_000_000, (parts,),
        [pltpu.VMEM((LANES, LANES), F32)] + rows,
    )
    received = lax.all_to_all(slot_inputs, "grp", split_axis=0, concat_axis=0, tiled=True)
    (produced,) = call(
        expert_kernel,
        [block],
        4 * slot_rows * width * expert_in.shape[2], 9_500_000,
        (
            received,
            pltpu.with_memory_space_constraint(w_in, pltpu.VMEM),
            pltpu.with_memory_space_constraint(w_out, pltpu.VMEM),
        ),
        rows,
    )
    returned = lax.all_to_all(
        produced, "grp", split_axis=0, concat_axis=0, tiled=True
    ).reshape(1, slot_rows, width)
    own = lax.all_to_all(
        jnp.broadcast_to(returned, (chips, slot_rows, width)),
        ("x", "y"), split_axis=0, concat_axis=0, tiled=True,
    ).reshape(half, width)
    other = lax.ppermute(own, "core", SWAP)
    own_w, other_w = call(
        softmax_kernel,
        [shape((count, half), BF16), shape((count, half), BF16)],
        slots * width * count, 4_000_000, (kept, other_q, logits),
    )
    mixed = dot(own_w, own) + dot(other_w, other)
    return mixed.astype(BF16)[None]


def solution(mesh):
    fine = Mesh(mesh.devices.reshape(4, 4, 2, 8), ("x", "y", "core", "grp"))
    ctx = ("x", "y", "core")
    in_specs = (
        P("grp", ctx, None),
        P(),
        P(ctx + ("grp",), None, None),
        P(ctx + ("grp",), None, None),
    )
    return jax.shard_map(
        per_device, mesh=fine, in_specs=in_specs, out_specs=P("grp", ctx, None), check_vma=False
    )
```

time: 80 us -> 77.3 us (0.966)
  Pallas kernels: 10.5 us -> 8.79 us
    pallas_call x5, Pallas kernels: 10.5 us -> 8.79 us  [call(): pl.pallas_call(body, out_shape=outs, in_specs=[pl.BlockSpec(memory_space=...]
  transfers between devices with their start and end apart: 2 -> 2, of which waited for: 1 -> 1; matrix products, arithmetic and copies ran while one was open for 1% -> 1% of each run, Pallas kernels for 7% -> 6%
where the time goes in v4:
time: 77.3 us; the launch traced here: 77 us
  blocking collectives  57.3 us (74%)
  Pallas kernels  8.79 us (11%)
  starting transfers between devices  8.3 us (11%)
  matrix products  2.31 us (3%)
    all_to_all x1, blocking collectives, per_device(): lax.all_to_all(packed, ('x', 'y'), split_axis=0, concat_axis=0, tiled=True)  18.7 us
    all_to_all x1, blocking collectives, per_device(): lax.all_to_all(slot_inputs, 'grp', split_axis=0, concat_axis=0, tiled=True)  15 us
    all_to_all x1, blocking collectives, per_device(): lax.all_to_all(jnp.broadcast_to(returned, (chips, slot_rows, width)), ('x...  14.1 us
    all_to_all x1, blocking collectives, per_device(): lax.all_to_all(produced, 'grp', split_axis=0, concat_axis=0, tiled=True)  9.42 us
    pallas_call x5, Pallas kernels, call(): pl.pallas_call(body, out_shape=outs, in_specs=[pl.BlockSpec(memory_space=...  8.79 us
    ppermute x1, starting transfers between devices, per_device(): other = lax.ppermute(own, 'core', SWAP)  5.06 us
    ppermute x1, starting transfers between devices, per_device(): x2 = lax.ppermute(x, 'core', SWAP)  3.24 us
    dot_general x2, matrix products, dot(): return lax.dot_general(a, b, dims, preferred_element_type=F32)  2.31 us
  transfers between devices with their start and end apart: 2, of which 1 were waited for; matrix products, arithmetic and copies ran while one was open for 1% of the time, Pallas kernels for 6%

profile of v4, /device:TPU:1, one launch (start us, length us, event | category | flops | bytes accessed | tf_op | source)
XLA Modules:
  0.0 77.0 jit_solution(18073191118516830491)
XLA Ops:
  0.0 3.2 %collective-permute-start = (bf16[640,768]{1,0:T(8,128)(2,1)}, bf16[640,768]{1,0:T(8,128)(2,1)S(1)}, u32[]{:S(2)}, u32[]{:S(2)}) collective-permute-start(bf16[640,768]{1,0:T(8,128)(2,1)} %bitcast.16), channel_id=1, source_target_pairs={{0,8},{8,0},{1,9},{9,1},{2,10},{10,2},{3,11},{11,3},{4,12},{12,4},... | collective-permute-start | bytes 2949128 | tf_op jit(solution)/shard_map/ppermute | solution.py:167
  3.2 0.0 slice-start
  3.2 3.3 %shard_map.46 = (bf16[768,512]{1,0:T(8,128)(2,1)S(1)}, bf16[768,512]{1,0:T(8,128)(2,1)S(1)}, bf16[640,768]{1,0:T(8,128)(2,1)S(1)}, f32[640,512]{1,0:T(8,128)S(1)}) custom-call(bf16[768,1024]{1,0:T(8,128)(2,1)} %q_hbm.1, bf16[640,768]{1,0:T(8,128)(2,1)} %bitcast.17), custom_call_target="tpu_custom_call" | custom-call | flops 1006632960 | bytes 5000000 | tf_op jit(solution)/shard_map/pallas_call | solution.py:24
  6.5 0.0 collective-permute-done.x2
  6.5 0.0 slice-start.1
  6.5 0.0 copy-start
  6.5 2.1 %shard_map.48 = bf16[16,208,128]{2,1,0:T(8,128)(2,1)S(1)} custom-call(bf16[768,512]{1,0:T(8,128)(2,1)S(1)} %get-tuple-element.15.own_q, bf16[640,768]{1,0:T(8,128)(2,1)S(1)} %get-tuple-element.11.x, bf16[640,768]{1,0:T(8,128)(2,1)S(1)} %collective-permute-done.x2, f32[640,512]{1,0:T(8,128)S(1)} %get-tuple-element.13.logits), custom_call_target="tpu_custom_call" | custom-call | flops 1509949440 | bytes 5000000 | tf_op jit(solution)/shard_map/pallas_call | solution.py:24
  8.7 18.7 %all_to_all.20.parts = bf16[16,208,128]{2,1,0:T(8,128)(2,1)S(1)} all-to-all(bf16[16,208,128]{2,1,0:T(8,128)(2,1)S(1)} %shard_map.48), channel_id=1, replica_groups=mesh['x'=4,'y'=4,'core'=2,'grp'=8] {'x','y'}, dimensions={0} | all-to-all | bytes 1703936 | tf_op jit(solution)/shard_map/all_to_all | solution.py:188
  27.4 0.4 shard_map.49
  27.8 15.0 %all_to_all.21.received = bf16[8,4,768]{2,1,0:T(4,128)(2,1)S(1)} all-to-all(bf16[8,4,768]{2,1,0:T(4,128)(2,1)S(1)} %shard_map.49), channel_id=1, replica_groups=mesh['x'=4,'y'=4,'core'=2,'grp'=8] {'grp'}, dimensions={0} | all-to-all | bytes 98304 | tf_op jit(solution)/shard_map/all_to_all | solution.py:197
  42.9 0.0 slice-done
  42.9 0.0 slice-done.1
  42.9 0.0 copy-done
  42.9 1.9 %shard_map.50 = bf16[8,4,768]{2,1,0:T(4,128)(2,1)S(1)} custom-call(bf16[8,4,768]{2,1,0:T(4,128)(2,1)S(1)} %all_to_all.21.received, bf16[768,3072]{1,0:T(8,128)(2,1)S(1)} %bitcast.12, bf16[3072,768]{1,0:T(8,128)(2,1)S(1)} %bitcast.13), custom_call_target="tpu_custom_call" | custom-call | flops 301989888 | bytes 9500000 | tf_op jit(solution)/shard_map/pallas_call | solution.py:24
  44.8 9.4 %all_to_all.22 = bf16[8,4,768]{2,1,0:T(4,128)(2,1)S(1)} all-to-all(bf16[8,4,768]{2,1,0:T(4,128)(2,1)S(1)} %shard_map.50), channel_id=1, replica_groups=mesh['x'=4,'y'=4,'core'=2,'grp'=8] {'grp'}, dimensions={0} | all-to-all | bytes 98304 | tf_op jit(solution)/shard_map/all_to_all | solution.py:209
  54.2 0.1 broadcast_in_dim.11
  54.3 14.1 %all_to_all.23 = bf16[16,32,768]{2,1,0:T(8,128)(2,1)S(1)} all-to-all(bf16[16,32,768]{2,1,0:T(8,128)(2,1)S(1)} %broadcast_in_dim.11), channel_id=1, replica_groups=mesh['x'=4,'y'=4,'core'=2,'grp'=8] {'x','y'}, dimensions={0} | all-to-all | bytes 1572864 | tf_op jit(solution)/shard_map/all_to_all | solution.py:212
  68.4 5.1 %collective-permute-start.1 = (bf16[512,768]{1,0:T(8,128)(2,1)S(1)}, bf16[512,768]{1,0:T(8,128)(2,1)S(1)}, u32[]{:S(2)}, u32[]{:S(2)}) collective-permute-start(bf16[512,768]{1,0:T(8,128)(2,1)S(1)} %bitcast.14), channel_id=1, source_target_pairs={{0,8},{8,0},{1,9},{9,1},{2,10},{10,2},{3,11},{11,3},{4,12},{12,4},... | collective-permute-start | bytes 2359304 | tf_op jit(solution)/shard_map/ppermute | solution.py:216
  73.5 1.1 %shard_map.47 = (bf16[640,512]{1,0:T(8,128)(2,1)S(1)}, bf16[640,512]{1,0:T(8,128)(2,1)S(1)}) custom-call(bf16[640,768]{1,0:T(8,128)(2,1)S(1)} %get-tuple-element.11.x, bf16[768,512]{1,0:T(8,128)(2,1)S(1)} %get-tuple-element.12.other_q, f32[640,512]{1,0:T(8,128)S(1)} %get-tuple-element.13.logits), custom_call_target="tpu_custom_call" | custom-call | flops 503316480 | bytes 4000000 | tf_op jit(solution)/shard_map/pallas_call | solution.py:24
  74.6 0.7 fusion.1
  75.3 0.1 collective-permute-done.1
  75.4 1.6 %fusion = bf16[1,640,768]{2,1,0:T(8,128)(2,1)} fusion(f32[640,768]{1,0:T(8,128)S(1)} %fusion.1, bf16[640,512]{1,0:T(8,128)(2,1)S(1)} %get-tuple-element.16, bf16[512,768]{1,0:T(8,128)(2,1)S(1)} %collective-permute-done.1), kind=kOutput, calls=%fused_computation.1 | convolution fusion | flops 504299520 | bytes 4390912 | tf_op jit(solution)/shard_map/dot_general | solution.py:20
  (2 shorter events, 0.0 us)
Async XLA Ops:
  0.0 6.5 %collective-permute-start = (bf16[640,768]{1,0:T(8,128)(2,1)}, bf16[640,768]{1,0:T(8,128)(2,1)S(1)}, u32[]{:S(2)}, u32[]{:S(2)}) collective-permute-start(bf16[640,768]{1,0:T(8,128)(2,1)} %bitcast.16), channel_id=1, source_target_pairs={{0,8},{8,0},{1,9},{9,1},{2,10},{10,2},{3,11},{11,3},{4,12},{12,4},... | collective-permute-start | bytes 2949128 | tf_op jit(solution)/shard_map/ppermute | solution.py:167
  3.2 39.6 %slice-start = ((s8[4718592]{0:T(1024)(128)(4,1)}), s8[4194304]{0:T(1024)(128)(4,1)S(1)}, s32[]{:S(2)}) async-start(s8[4718592]{0:T(1024)(128)(4,1)} %bitcast.10), calls=%async_computation.4 | async-start | bytes 8388608
  6.5 36.4 %slice-start.1 = ((s8[4718592]{0:T(1024)(128)(4,1)}), s8[524288]{0:T(1024)(128)(4,1)S(1)}, s32[]{:S(2)}) async-start(s8[4718592]{0:T(1024)(128)(4,1)} %bitcast.10), calls=%async_computation.5 | async-start | bytes 1048576
  6.5 36.3 %copy-start = (bf16[1,3072,768]{2,1,0:T(8,128)(2,1)S(1)}, bf16[1,3072,768]{2,1,0:T(8,128)(2,1)}, u32[]{:S(2)}) copy-start(bf16[1,3072,768]{2,1,0:T(8,128)(2,1)} %param.7) | copy-start | bytes 14155780
  68.4 7.0 %collective-permute-start.1 = (bf16[512,768]{1,0:T(8,128)(2,1)S(1)}, bf16[512,768]{1,0:T(8,128)(2,1)S(1)}, u32[]{:S(2)}, u32[]{:S(2)}) collective-permute-start(bf16[512,768]{1,0:T(8,128)(2,1)S(1)} %bitcast.14), channel_id=1, source_target_pairs={{0,8},{8,0},{1,9},{9,1},{2,10},{10,2},{3,11},{11,3},{4,12},{12,4},... | collective-permute-start | bytes 2359304 | tf_op jit(solution)/shard_map/ppermute | solution.py:216

commit v5 on v4

--- a/solution.py
+++ b/solution.py
@@ -13,6 +13,7 @@
 LIMIT = 24 * 1024 * 1024
 LANES = 128
 TAIL = 16
+CHUNKS = 2
 OVER_ROWS = (((0,), (0,)), ((), ()))
 
 
@@ -39,14 +40,13 @@
 def logit_kernel(slot_rows, q_hbm, x_hbm, own_q, other_q, x, logits, q, sems):
     group = 256
     kept = group // 2
-    blocks = q.shape[1] // group
-    loads = []
-    for b in range(blocks):
-        columns = slice(b * group, (b + 1) * group)
-        loads.append(
-            pltpu.make_async_copy(q_hbm.at[:, columns], q.at[:, columns], sems.at[b])
-        )
-    loads.append(pltpu.make_async_copy(x_hbm, x, sems.at[blocks]))
+    chunk = q.shape[0] // CHUNKS
+    chunks = [slice(i * chunk, (i + 1) * chunk) for i in range(CHUNKS)]
+    loads = [
+        pltpu.make_async_copy(q_hbm.at[rows, :], q.at[rows, :], sems.at[i])
+        for i, rows in enumerate(chunks)
+    ]
+    loads.append(pltpu.make_async_copy(x_hbm, x, sems.at[CHUNKS]))
     for load in loads:
         load.start()
     core = lax.axis_index("core")
@@ -57,13 +57,14 @@
     column = column % kept
     place = column // slot_rows * pair + column % slot_rows + (kind ^ core) * slot_rows
     pick = jnp.where(row == place, 1.0, 0.0).astype(BF16)
-    for b in range(blocks):
-        loads[b].wait()
-        picked = dot(q[:, b * group : (b + 1) * group], pick).astype(BF16)
-        columns = slice(b * kept, (b + 1) * kept)
-        own_q[:, columns] = picked[:, :kept]
-        other_q[:, columns] = picked[:, kept:]
-    loads[blocks].wait()
+    for load, rows in zip(loads, chunks):
+        load.wait()
+        for b in range(q.shape[1] // group):
+            picked = dot(q[rows, b * group : (b + 1) * group], pick).astype(BF16)
+            columns = slice(b * kept, (b + 1) * kept)
+            own_q[rows, columns] = picked[:, :kept]
+            other_q[rows, columns] = picked[:, kept:]
+    loads[CHUNKS].wait()
     logits[...] = dot(x[...], own_q[...])
 
 
@@ -144,14 +145,8 @@
     for g in range(groups):
         scratch[g * held : (g + 1) * held, :] = received[g].astype(F32)
     x = scratch[...].astype(BF16)
-    hidden = w_in.shape[1]
-    step = 768
-    acc = jnp.zeros(scratch.shape, F32)
-    for start in range(0, hidden, step):
-        part = slice(start, start + step)
-        h = jax.nn.gelu(dot(x, w_in[:, part]), approximate=True).astype(BF16)
-        acc = acc + dot(h, w_out[part, :])
-    scratch[...] = acc
+    h = jax.nn.gelu(dot(x, w_in[...]), approximate=True).astype(BF16)
+    scratch[...] = dot(h, w_out[...])
     for g in range(groups):
         out[g] = scratch[g * held : (g + 1) * held, :].astype(BF16)
 
@@ -176,7 +171,7 @@
         ],
         2 * slots * width * count, 5_000_000,
         [pltpu.with_memory_space_constraint(a, pltpu.HBM) for a in (slot_query, x)],
-        [pltpu.VMEM((width, slots), BF16), pltpu.SemaphoreType.DMA((5,))],
+        [pltpu.VMEM((width, slots), BF16), pltpu.SemaphoreType.DMA((CHUNKS + 1,))],
         pl.ANY,
     )
     (packed,) = call(

time: 77.3 us -> 76.6 us (level)
  transfers between devices with their start and end apart: 2 -> 2, of which waited for: 1 -> 1; matrix products, arithmetic and copies ran while one was open for 1% -> 1% of each run, Pallas kernels for 6% -> 5%
where the time goes in v5:
time: 76.6 us; the launch traced here: 76.4 us
  blocking collectives  57.3 us (75%)
  starting transfers between devices  8.3 us (11%)
  Pallas kernels  8.13 us (11%)
  matrix products  2.31 us (3%)
    all_to_all x1, blocking collectives, per_device(): lax.all_to_all(packed, ('x', 'y'), split_axis=0, concat_axis=0, tiled=True)  18.8 us
    all_to_all x1, blocking collectives, per_device(): lax.all_to_all(slot_inputs, 'grp', split_axis=0, concat_axis=0, tiled=True)  15 us
    all_to_all x1, blocking collectives, per_device(): lax.all_to_all(jnp.broadcast_to(returned, (chips, slot_rows, width)), ('x...  14.1 us
    all_to_all x1, blocking collectives, per_device(): lax.all_to_all(produced, 'grp', split_axis=0, concat_axis=0, tiled=True)  9.42 us
    pallas_call x5, Pallas kernels, call(): pl.pallas_call(body, out_shape=outs, in_specs=[pl.BlockSpec(memory_space=...  8.13 us
    ppermute x1, starting transfers between devices, per_device(): other = lax.ppermute(own, 'core', SWAP)  5.06 us
    ppermute x1, starting transfers between devices, per_device(): x2 = lax.ppermute(x, 'core', SWAP)  3.24 us
    dot_general x2, matrix products, dot(): return lax.dot_general(a, b, dims, preferred_element_type=F32)  2.31 us
  transfers between devices with their start and end apart: 2, of which 1 were waited for; matrix products, arithmetic and copies ran while one was open for 1% of the time, Pallas kernels for 5%

profile of v5, /device:TPU:1, one launch (start us, length us, event | category | flops | bytes accessed | tf_op | source)
XLA Modules:
  0.0 76.4 jit_solution(11285327600519784181)
XLA Ops:
  0.0 3.2 %collective-permute-start = (bf16[640,768]{1,0:T(8,128)(2,1)}, bf16[640,768]{1,0:T(8,128)(2,1)S(1)}, u32[]{:S(2)}, u32[]{:S(2)}) collective-permute-start(bf16[640,768]{1,0:T(8,128)(2,1)} %bitcast.16), channel_id=1, source_target_pairs={{0,8},{8,0},{1,9},{9,1},{2,10},{10,2},{3,11},{11,3},{4,12},{12,4},... | collective-permute-start | bytes 2949128 | tf_op jit(solution)/shard_map/ppermute | solution.py:162
  3.2 0.0 slice-start
  3.2 2.7 %shard_map.46 = (bf16[768,512]{1,0:T(8,128)(2,1)S(1)}, bf16[768,512]{1,0:T(8,128)(2,1)S(1)}, bf16[640,768]{1,0:T(8,128)(2,1)S(1)}, f32[640,512]{1,0:T(8,128)S(1)}) custom-call(bf16[768,1024]{1,0:T(8,128)(2,1)} %q_hbm.1, bf16[640,768]{1,0:T(8,128)(2,1)} %bitcast.17), custom_call_target="tpu_custom_call" | custom-call | flops 1006632960 | bytes 5000000 | tf_op jit(solution)/shard_map/pallas_call | solution.py:25
  6.0 0.0 collective-permute-done.x2
  6.0 0.0 slice-start.1
  6.0 0.0 copy-start
  6.0 2.1 %shard_map.48 = bf16[16,208,128]{2,1,0:T(8,128)(2,1)S(1)} custom-call(bf16[768,512]{1,0:T(8,128)(2,1)S(1)} %get-tuple-element.15.own_q, bf16[640,768]{1,0:T(8,128)(2,1)S(1)} %get-tuple-element.11.x, bf16[640,768]{1,0:T(8,128)(2,1)S(1)} %collective-permute-done.x2, f32[640,512]{1,0:T(8,128)S(1)} %get-tuple-element.13.logits), custom_call_target="tpu_custom_call" | custom-call | flops 1509949440 | bytes 5000000 | tf_op jit(solution)/shard_map/pallas_call | solution.py:25
  8.2 18.8 %all_to_all.20.parts = bf16[16,208,128]{2,1,0:T(8,128)(2,1)S(1)} all-to-all(bf16[16,208,128]{2,1,0:T(8,128)(2,1)S(1)} %shard_map.48), channel_id=1, replica_groups=mesh['x'=4,'y'=4,'core'=2,'grp'=8] {'x','y'}, dimensions={0} | all-to-all | bytes 1703936 | tf_op jit(solution)/shard_map/all_to_all | solution.py:183
  26.9 0.4 shard_map.49
  27.3 15.0 %all_to_all.21.received = bf16[8,4,768]{2,1,0:T(4,128)(2,1)S(1)} all-to-all(bf16[8,4,768]{2,1,0:T(4,128)(2,1)S(1)} %shard_map.49), channel_id=1, replica_groups=mesh['x'=4,'y'=4,'core'=2,'grp'=8] {'grp'}, dimensions={0} | all-to-all | bytes 98304 | tf_op jit(solution)/shard_map/all_to_all | solution.py:192
  42.4 0.0 slice-done
  42.4 0.0 slice-done.1
  42.4 0.0 copy-done
  42.4 1.8 %shard_map.50 = bf16[8,4,768]{2,1,0:T(4,128)(2,1)S(1)} custom-call(bf16[8,4,768]{2,1,0:T(4,128)(2,1)S(1)} %all_to_all.21.received, bf16[768,3072]{1,0:T(8,128)(2,1)S(1)} %bitcast.12, bf16[3072,768]{1,0:T(8,128)(2,1)S(1)} %bitcast.13), custom_call_target="tpu_custom_call" | custom-call | flops 301989888 | bytes 9500000 | tf_op jit(solution)/shard_map/pallas_call | solution.py:25
  44.1 9.4 %all_to_all.22 = bf16[8,4,768]{2,1,0:T(4,128)(2,1)S(1)} all-to-all(bf16[8,4,768]{2,1,0:T(4,128)(2,1)S(1)} %shard_map.50), channel_id=1, replica_groups=mesh['x'=4,'y'=4,'core'=2,'grp'=8] {'grp'}, dimensions={0} | all-to-all | bytes 98304 | tf_op jit(solution)/shard_map/all_to_all | solution.py:204
  53.6 0.1 broadcast_in_dim.11
  53.7 14.1 %all_to_all.23 = bf16[16,32,768]{2,1,0:T(8,128)(2,1)S(1)} all-to-all(bf16[16,32,768]{2,1,0:T(8,128)(2,1)S(1)} %broadcast_in_dim.11), channel_id=1, replica_groups=mesh['x'=4,'y'=4,'core'=2,'grp'=8] {'x','y'}, dimensions={0} | all-to-all | bytes 1572864 | tf_op jit(solution)/shard_map/all_to_all | solution.py:207
  67.8 5.1 %collective-permute-start.1 = (bf16[512,768]{1,0:T(8,128)(2,1)S(1)}, bf16[512,768]{1,0:T(8,128)(2,1)S(1)}, u32[]{:S(2)}, u32[]{:S(2)}) collective-permute-start(bf16[512,768]{1,0:T(8,128)(2,1)S(1)} %bitcast.14), channel_id=1, source_target_pairs={{0,8},{8,0},{1,9},{9,1},{2,10},{10,2},{3,11},{11,3},{4,12},{12,4},... | collective-permute-start | bytes 2359304 | tf_op jit(solution)/shard_map/ppermute | solution.py:211
  72.8 1.1 %shard_map.47 = (bf16[640,512]{1,0:T(8,128)(2,1)S(1)}, bf16[640,512]{1,0:T(8,128)(2,1)S(1)}) custom-call(bf16[640,768]{1,0:T(8,128)(2,1)S(1)} %get-tuple-element.11.x, bf16[768,512]{1,0:T(8,128)(2,1)S(1)} %get-tuple-element.12.other_q, f32[640,512]{1,0:T(8,128)S(1)} %get-tuple-element.13.logits), custom_call_target="tpu_custom_call" | custom-call | flops 503316480 | bytes 4000000 | tf_op jit(solution)/shard_map/pallas_call | solution.py:25
  74.0 0.7 fusion.1
  74.6 0.1 collective-permute-done.1
  74.7 1.6 %fusion = bf16[1,640,768]{2,1,0:T(8,128)(2,1)} fusion(f32[640,768]{1,0:T(8,128)S(1)} %fusion.1, bf16[640,512]{1,0:T(8,128)(2,1)S(1)} %get-tuple-element.16, bf16[512,768]{1,0:T(8,128)(2,1)S(1)} %collective-permute-done.1), kind=kOutput, calls=%fused_computation.1 | convolution fusion | flops 504299520 | bytes 4390912 | tf_op jit(solution)/shard_map/dot_general | solution.py:21
  (2 shorter events, 0.0 us)
Async XLA Ops:
  0.0 6.0 %collective-permute-start = (bf16[640,768]{1,0:T(8,128)(2,1)}, bf16[640,768]{1,0:T(8,128)(2,1)S(1)}, u32[]{:S(2)}, u32[]{:S(2)}) collective-permute-start(bf16[640,768]{1,0:T(8,128)(2,1)} %bitcast.16), channel_id=1, source_target_pairs={{0,8},{8,0},{1,9},{9,1},{2,10},{10,2},{3,11},{11,3},{4,12},{12,4},... | collective-permute-start | bytes 2949128 | tf_op jit(solution)/shard_map/ppermute | solution.py:162
  3.2 39.1 %slice-start = ((s8[4718592]{0:T(1024)(128)(4,1)}), s8[4194304]{0:T(1024)(128)(4,1)S(1)}, s32[]{:S(2)}) async-start(s8[4718592]{0:T(1024)(128)(4,1)} %bitcast.10), calls=%async_computation.4 | async-start | bytes 8388608
  6.0 36.4 %slice-start.1 = ((s8[4718592]{0:T(1024)(128)(4,1)}), s8[524288]{0:T(1024)(128)(4,1)S(1)}, s32[]{:S(2)}) async-start(s8[4718592]{0:T(1024)(128)(4,1)} %bitcast.10), calls=%async_computation.5 | async-start | bytes 1048576
  6.0 36.4 %copy-start = (bf16[1,3072,768]{2,1,0:T(8,128)(2,1)S(1)}, bf16[1,3072,768]{2,1,0:T(8,128)(2,1)}, u32[]{:S(2)}) copy-start(bf16[1,3072,768]{2,1,0:T(8,128)(2,1)} %param.7) | copy-start | bytes 14155780
  67.8 7.0 %collective-permute-start.1 = (bf16[512,768]{1,0:T(8,128)(2,1)S(1)}, bf16[512,768]{1,0:T(8,128)(2,1)S(1)}, u32[]{:S(2)}, u32[]{:S(2)}) collective-permute-start(bf16[512,768]{1,0:T(8,128)(2,1)S(1)} %bitcast.14), channel_id=1, source_target_pairs={{0,8},{8,0},{1,9},{9,1},{2,10},{10,2},{3,11},{11,3},{4,12},{12,4},... | collective-permute-start | bytes 2359304 | tf_op jit(solution)/shard_map/ppermute | solution.py:211

commit v6 on v5

--- a/solution.py
+++ b/solution.py
@@ -14,6 +14,7 @@
 LANES = 128
 TAIL = 16
 CHUNKS = 2
+PIECES = 4
 OVER_ROWS = (((0,), (0,)), ((), ()))
 
 
@@ -21,12 +22,12 @@
     return lax.dot_general(a, b, dims, preferred_element_type=F32)
 
 
-def call(body, outs, flops, moved, args, scratch=(), space=pltpu.VMEM):
+def call(body, outs, flops, moved, args, scratch=(), space=pltpu.VMEM, to=pltpu.VMEM):
     return pl.pallas_call(
         body,
         out_shape=outs,
         in_specs=[pl.BlockSpec(memory_space=space)] * len(args),
-        out_specs=[pl.BlockSpec(memory_space=pltpu.VMEM)] * len(outs),
+        out_specs=[pl.BlockSpec(memory_space=to)] * len(outs),
         scratch_shapes=list(scratch),
         compiler_params=pltpu.CompilerParams(vmem_limit_bytes=LIMIT),
         cost_estimate=pl.CostEstimate(flops=flops, bytes_accessed=moved, transcendentals=0),
@@ -151,6 +152,18 @@
         out[g] = scratch[g * held : (g + 1) * held, :].astype(BF16)
 
 
+def final_kernel(partial, weights, rows, out, buffer, sems):
+    count = buffer.shape[0] // PIECES
+    stores = []
+    for i in range(PIECES):
+        part = slice(i * count, (i + 1) * count)
+        buffer[part, :] = (partial[part, :] + dot(weights[part, :], rows[...])).astype(BF16)
+        stores.append(pltpu.make_async_copy(buffer.at[part, :], out.at[part, :], sems.at[i]))
+        stores[i].start()
+    for store in stores:
+        store.wait()
+
+
 def per_device(tokens, slot_query, expert_in, expert_out):
     x = tokens[0]
     count, width = x.shape
@@ -214,8 +227,14 @@
         [shape((count, half), BF16), shape((count, half), BF16)],
         slots * width * count, 4_000_000, (kept, other_q, logits),
     )
-    mixed = dot(own_w, own) + dot(other_w, other)
-    return mixed.astype(BF16)[None]
+    (mixed,) = call(
+        final_kernel,
+        [shape((count, width), BF16)],
+        slots * width * count, 4_000_000, (dot(own_w, own), other_w, other),
+        [pltpu.VMEM((count, width), BF16), pltpu.SemaphoreType.DMA((PIECES,))],
+        to=pl.ANY,
+    )
+    return mixed[None]
 
 
 def solution(mesh):

time: 76.6 us -> 76.4 us (level)
  matrix products: 2.31 us -> 0.67 us
  Pallas kernels: 8.13 us -> 9.54 us
    dot_general x2 -> x1, matrix products: 2.31 us -> 0.67 us  [dot(): return lax.dot_general(a, b, dims, preferred_element_type=F32)]
    pallas_call x5 -> x6, Pallas kernels: 8.13 us -> 9.54 us  [call(): pl.pallas_call(body, out_shape=outs, in_specs=[pl.BlockSpec(memory_space=...]
where the time goes in v6:
time: 76.4 us; the launch traced here: 76.2 us
  blocking collectives  57.3 us (75%)
  Pallas kernels  9.54 us (12%)
  starting transfers between devices  8.3 us (11%)
    all_to_all x1, blocking collectives, per_device(): lax.all_to_all(packed, ('x', 'y'), split_axis=0, concat_axis=0, tiled=True)  18.8 us
    all_to_all x1, blocking collectives, per_device(): lax.all_to_all(slot_inputs, 'grp', split_axis=0, concat_axis=0, tiled=True)  15 us
    all_to_all x1, blocking collectives, per_device(): lax.all_to_all(jnp.broadcast_to(returned, (chips, slot_rows, width)), ('x...  14.1 us
    pallas_call x6, Pallas kernels, call(): pl.pallas_call(body, out_shape=outs, in_specs=[pl.BlockSpec(memory_space=...  9.54 us
    all_to_all x1, blocking collectives, per_device(): lax.all_to_all(produced, 'grp', split_axis=0, concat_axis=0, tiled=True)  9.42 us
    ppermute x1, starting transfers between devices, per_device(): other = lax.ppermute(own, 'core', SWAP)  5.06 us
    ppermute x1, starting transfers between devices, per_device(): x2 = lax.ppermute(x, 'core', SWAP)  3.24 us
  transfers between devices with their start and end apart: 2, of which 1 were waited for; matrix products, arithmetic and copies ran while one was open for 1% of the time, Pallas kernels for 5%

profile of v6, /device:TPU:1, one launch (start us, length us, event | category | flops | bytes accessed | tf_op | source)
XLA Modules:
  0.0 76.2 jit_solution(2474842225290745178)
XLA Ops:
  0.0 3.2 %collective-permute-start = (bf16[640,768]{1,0:T(8,128)(2,1)}, bf16[640,768]{1,0:T(8,128)(2,1)S(1)}, u32[]{:S(2)}, u32[]{:S(2)}) collective-permute-start(bf16[640,768]{1,0:T(8,128)(2,1)} %bitcast.13), channel_id=1, source_target_pairs={{0,8},{8,0},{1,9},{9,1},{2,10},{10,2},{3,11},{11,3},{4,12},{12,4},... | collective-permute-start | bytes 2949128 | tf_op jit(solution)/shard_map/ppermute | solution.py:175
  3.2 0.0 slice-start
  3.2 2.7 %shard_map.46 = (bf16[768,512]{1,0:T(8,128)(2,1)S(1)}, bf16[768,512]{1,0:T(8,128)(2,1)S(1)}, bf16[640,768]{1,0:T(8,128)(2,1)S(1)}, f32[640,512]{1,0:T(8,128)S(1)}) custom-call(bf16[768,1024]{1,0:T(8,128)(2,1)} %q_hbm.1, bf16[640,768]{1,0:T(8,128)(2,1)} %bitcast.14), custom_call_target="tpu_custom_call" | custom-call | flops 1006632960 | bytes 5000000 | tf_op jit(solution)/shard_map/pallas_call | solution.py:26
  6.0 0.0 collective-permute-done.x2
  6.0 0.0 slice-start.1
  6.0 0.0 copy-start
  6.0 2.1 %shard_map.48 = bf16[16,208,128]{2,1,0:T(8,128)(2,1)S(1)} custom-call(bf16[768,512]{1,0:T(8,128)(2,1)S(1)} %get-tuple-element.15.own_q, bf16[640,768]{1,0:T(8,128)(2,1)S(1)} %get-tuple-element.11.x, bf16[640,768]{1,0:T(8,128)(2,1)S(1)} %collective-permute-done.x2, f32[640,512]{1,0:T(8,128)S(1)} %get-tuple-element.13.logits), custom_call_target="tpu_custom_call" | custom-call | flops 1509949440 | bytes 5000000 | tf_op jit(solution)/shard_map/pallas_call | solution.py:26
  8.2 18.8 %all_to_all.20.parts = bf16[16,208,128]{2,1,0:T(8,128)(2,1)S(1)} all-to-all(bf16[16,208,128]{2,1,0:T(8,128)(2,1)S(1)} %shard_map.48), channel_id=1, replica_groups=mesh['x'=4,'y'=4,'core'=2,'grp'=8] {'x','y'}, dimensions={0} | all-to-all | bytes 1703936 | tf_op jit(solution)/shard_map/all_to_all | solution.py:196
  26.9 0.4 shard_map.49
  27.3 15.0 %all_to_all.21.received = bf16[8,4,768]{2,1,0:T(4,128)(2,1)S(1)} all-to-all(bf16[8,4,768]{2,1,0:T(4,128)(2,1)S(1)} %shard_map.49), channel_id=1, replica_groups=mesh['x'=4,'y'=4,'core'=2,'grp'=8] {'grp'}, dimensions={0} | all-to-all | bytes 98304 | tf_op jit(solution)/shard_map/all_to_all | solution.py:205
  42.4 0.0 slice-done
  42.4 0.0 slice-done.1
  42.4 0.0 copy-done
  42.4 1.8 %shard_map.50 = bf16[8,4,768]{2,1,0:T(4,128)(2,1)S(1)} custom-call(bf16[8,4,768]{2,1,0:T(4,128)(2,1)S(1)} %all_to_all.21.received, bf16[768,3072]{1,0:T(8,128)(2,1)S(1)} %bitcast.9, bf16[3072,768]{1,0:T(8,128)(2,1)S(1)} %bitcast.10), custom_call_target="tpu_custom_call" | custom-call | flops 301989888 | bytes 9500000 | tf_op jit(solution)/shard_map/pallas_call | solution.py:26
  44.1 9.4 %all_to_all.22 = bf16[8,4,768]{2,1,0:T(4,128)(2,1)S(1)} all-to-all(bf16[8,4,768]{2,1,0:T(4,128)(2,1)S(1)} %shard_map.50), channel_id=1, replica_groups=mesh['x'=4,'y'=4,'core'=2,'grp'=8] {'grp'}, dimensions={0} | all-to-all | bytes 98304 | tf_op jit(solution)/shard_map/all_to_all | solution.py:217
  53.6 0.1 broadcast_in_dim.11
  53.7 14.1 %all_to_all.23 = bf16[16,32,768]{2,1,0:T(8,128)(2,1)S(1)} all-to-all(bf16[16,32,768]{2,1,0:T(8,128)(2,1)S(1)} %broadcast_in_dim.11), channel_id=1, replica_groups=mesh['x'=4,'y'=4,'core'=2,'grp'=8] {'x','y'}, dimensions={0} | all-to-all | bytes 1572864 | tf_op jit(solution)/shard_map/all_to_all | solution.py:220
  67.8 5.1 %collective-permute-start.1 = (bf16[512,768]{1,0:T(8,128)(2,1)S(1)}, bf16[512,768]{1,0:T(8,128)(2,1)S(1)}, u32[]{:S(2)}, u32[]{:S(2)}) collective-permute-start(bf16[512,768]{1,0:T(8,128)(2,1)S(1)} %bitcast.11), channel_id=1, source_target_pairs={{0,8},{8,0},{1,9},{9,1},{2,10},{10,2},{3,11},{11,3},{4,12},{12,4},... | collective-permute-start | bytes 2359304 | tf_op jit(solution)/shard_map/ppermute | solution.py:224
  72.8 1.1 %shard_map.47 = (bf16[640,512]{1,0:T(8,128)(2,1)S(1)}, bf16[640,512]{1,0:T(8,128)(2,1)S(1)}) custom-call(bf16[640,768]{1,0:T(8,128)(2,1)S(1)} %get-tuple-element.11.x, bf16[768,512]{1,0:T(8,128)(2,1)S(1)} %get-tuple-element.12.other_q, f32[640,512]{1,0:T(8,128)S(1)} %get-tuple-element.13.logits), custom_call_target="tpu_custom_call" | custom-call | flops 503316480 | bytes 4000000 | tf_op jit(solution)/shard_map/pallas_call | solution.py:26
  74.0 0.7 fusion.partial
  74.6 0.1 collective-permute-done.1.rows
  74.7 1.4 %shard_map.51 = bf16[640,768]{1,0:T(8,128)(2,1)} custom-call(f32[640,768]{1,0:T(8,128)S(1)} %fusion.partial, bf16[640,512]{1,0:T(8,128)(2,1)S(1)} %get-tuple-element.16.weights, bf16[512,768]{1,0:T(8,128)(2,1)S(1)} %collective-permute-done.1.rows), custom_call_target="tpu_custom_call" | custom-call | flops 503316480 | bytes 4000000 | tf_op jit(solution)/shard_map/pallas_call | solution.py:26
  (2 shorter events, 0.0 us)
Async XLA Ops:
  0.0 6.0 %collective-permute-start = (bf16[640,768]{1,0:T(8,128)(2,1)}, bf16[640,768]{1,0:T(8,128)(2,1)S(1)}, u32[]{:S(2)}, u32[]{:S(2)}) collective-permute-start(bf16[640,768]{1,0:T(8,128)(2,1)} %bitcast.13), channel_id=1, source_target_pairs={{0,8},{8,0},{1,9},{9,1},{2,10},{10,2},{3,11},{11,3},{4,12},{12,4},... | collective-permute-start | bytes 2949128 | tf_op jit(solution)/shard_map/ppermute | solution.py:175
  3.2 39.1 %slice-start = ((s8[4718592]{0:T(1024)(128)(4,1)}), s8[4194304]{0:T(1024)(128)(4,1)S(1)}, s32[]{:S(2)}) async-start(s8[4718592]{0:T(1024)(128)(4,1)} %bitcast.7), calls=%async_computation.4 | async-start | bytes 8388608
  6.0 36.4 %slice-start.1 = ((s8[4718592]{0:T(1024)(128)(4,1)}), s8[524288]{0:T(1024)(128)(4,1)S(1)}, s32[]{:S(2)}) async-start(s8[4718592]{0:T(1024)(128)(4,1)} %bitcast.7), calls=%async_computation.5 | async-start | bytes 1048576
  6.0 36.4 %copy-start = (bf16[1,3072,768]{2,1,0:T(8,128)(2,1)S(1)}, bf16[1,3072,768]{2,1,0:T(8,128)(2,1)}, u32[]{:S(2)}) copy-start(bf16[1,3072,768]{2,1,0:T(8,128)(2,1)} %param.7) | copy-start | bytes 14155780
  67.8 7.0 %collective-permute-start.1 = (bf16[512,768]{1,0:T(8,128)(2,1)S(1)}, bf16[512,768]{1,0:T(8,128)(2,1)S(1)}, u32[]{:S(2)}, u32[]{:S(2)}) collective-permute-start(bf16[512,768]{1,0:T(8,128)(2,1)S(1)} %bitcast.11), channel_id=1, source_target_pairs={{0,8},{8,0},{1,9},{9,1},{2,10},{10,2},{3,11},{11,3},{4,12},{12,4},... | collective-permute-start | bytes 2359304 | tf_op jit(solution)/shard_map/ppermute | solution.py:224

commit v7 on v6

--- a/solution.py
+++ b/solution.py
@@ -10,11 +10,13 @@
 BF16 = jnp.bfloat16
 F32 = jnp.float32
 SWAP = [(0, 1), (1, 0)]
+CTX = ("x", "y", "core")
 LIMIT = 24 * 1024 * 1024
 LANES = 128
 TAIL = 16
 CHUNKS = 2
 PIECES = 4
+TURN_X, TURN_Y, TURN_Z = 2, 2, 4
 OVER_ROWS = (((0,), (0,)), ((), ()))
 
 
@@ -38,7 +40,7 @@
     return jnp.max(logits, axis=0, keepdims=True).astype(BF16).astype(F32)
 
 
-def logit_kernel(slot_rows, q_hbm, x_hbm, own_q, other_q, x, logits, q, sems):
+def logit_kernel(slot_rows, turn, q_hbm, x_hbm, own_q, other_q, x, logits, q, sems):
     group = 256
     kept = group // 2
     chunk = q.shape[0] // CHUNKS
@@ -56,13 +58,16 @@
     column = lax.broadcasted_iota(jnp.int32, (group, group), 1)
     kind = column // kept
     column = column % kept
-    place = column // slot_rows * pair + column % slot_rows + (kind ^ core) * slot_rows
+    chip = (column // slot_rows + TURN_Y) % (kept // slot_rows)
+    place = chip * pair + (column + turn) % slot_rows + (kind ^ core) * slot_rows
     pick = jnp.where(row == place, 1.0, 0.0).astype(BF16)
     for load, rows in zip(loads, chunks):
         load.wait()
-        for b in range(q.shape[1] // group):
+        blocks = q.shape[1] // group
+        for b in range(blocks):
             picked = dot(q[rows, b * group : (b + 1) * group], pick).astype(BF16)
-            columns = slice(b * kept, (b + 1) * kept)
+            place = (b - TURN_X) % blocks
+            columns = slice(place * kept, (place + 1) * kept)
             own_q[rows, columns] = picked[:, :kept]
             other_q[rows, columns] = picked[:, kept:]
     loads[CHUNKS].wait()
@@ -128,8 +133,8 @@
     weight = jnp.exp(top - jnp.max(top, axis=0, keepdims=True))
     weight = weight / jnp.sum(total * weight, axis=0, keepdims=True)
     weights[...] = weight.T
-    chip = lax.axis_index("x") * lax.axis_size("y") + lax.axis_index("y")
-    start = pl.multiple_of(chip % (LANES // held) * held, held)
+    place = (lax.axis_index("y") - TURN_Y) % (LANES // held)
+    start = pl.multiple_of(place * held, held)
     mine = weights[pl.ds(start, held), :]
     for j in range(width // LANES):
         part = slice(j * LANES, (j + 1) * LANES)
@@ -162,6 +167,22 @@
         stores[i].start()
     for store in stores:
         store.wait()
+
+
+def turned(size, turn):
+    return [(i + turn) % size for i in range(size)]
+
+
+def plane_groups(by_row=False):
+    xs, ys = turned(lax.axis_size("x"), TURN_X), turned(lax.axis_size("y"), TURN_Y)
+    order = [(x, y) for y in ys for x in xs] if by_row else [(x, y) for x in xs for y in ys]
+    return [[(x * len(ys) + y) * 2 + core for x, y in order] for core in range(2)]
+
+
+def exchange(values, axes, groups):
+    return lax.all_to_all(
+        values, axes, split_axis=0, concat_axis=0, tiled=True, axis_index_groups=groups
+    )
 
 
 def per_device(tokens, slot_query, expert_in, expert_out):
@@ -175,7 +196,7 @@
     x2 = lax.ppermute(x, "core", SWAP)
     shape = jax.ShapeDtypeStruct
     own_q, other_q, kept, logits = call(
-        functools.partial(logit_kernel, slot_rows),
+        functools.partial(logit_kernel, slot_rows, slot_rows // grp_count * TURN_Z),
         [
             shape((width, half), BF16),
             shape((width, half), BF16),
@@ -193,16 +214,15 @@
         3 * slots * width * count, 5_000_000, (own_q, kept, x2, logits),
     )
     w_in, w_out = expert_in[0], expert_out[0]
-    parts = lax.all_to_all(
-        packed, ("x", "y"), split_axis=0, concat_axis=0, tiled=True
-    )
+    parts = exchange(packed, CTX, plane_groups())
     block = shape((grp_count, slot_rows // grp_count, width), BF16)
     rows = [pltpu.VMEM((slot_rows, width), F32)]
     (slot_inputs,) = call(
         combine_kernel, [block], 2 * half * width, 1_000_000, (parts,),
         [pltpu.VMEM((LANES, LANES), F32)] + rows,
     )
-    received = lax.all_to_all(slot_inputs, "grp", split_axis=0, concat_axis=0, tiled=True)
+    line = [turned(grp_count, TURN_Z)]
+    received = exchange(slot_inputs, "grp", line)
     (produced,) = call(
         expert_kernel,
         [block],
@@ -214,13 +234,9 @@
         ),
         rows,
     )
-    returned = lax.all_to_all(
-        produced, "grp", split_axis=0, concat_axis=0, tiled=True
-    ).reshape(1, slot_rows, width)
-    own = lax.all_to_all(
-        jnp.broadcast_to(returned, (chips, slot_rows, width)),
-        ("x", "y"), split_axis=0, concat_axis=0, tiled=True,
-    ).reshape(half, width)
+    returned = exchange(produced, "grp", line).reshape(1, slot_rows, width)
+    copies = jnp.broadcast_to(returned, (chips, slot_rows, width))
+    own = exchange(copies, CTX, plane_groups()).reshape(half, width)
     other = lax.ppermute(own, "core", SWAP)
     own_w, other_w = call(
         softmax_kernel,
@@ -239,13 +255,12 @@
 
 def solution(mesh):
     fine = Mesh(mesh.devices.reshape(4, 4, 2, 8), ("x", "y", "core", "grp"))
-    ctx = ("x", "y", "core")
     in_specs = (
-        P("grp", ctx, None),
+        P("grp", CTX, None),
         P(),
-        P(ctx + ("grp",), None, None),
-        P(ctx + ("grp",), None, None),
+        P(CTX + ("grp",), None, None),
+        P(CTX + ("grp",), None, None),
     )
     return jax.shard_map(
-        per_device, mesh=fine, in_specs=in_specs, out_specs=P("grp", ctx, None), check_vma=False
-    )
+        per_device, mesh=fine, in_specs=in_specs, out_specs=P("grp", CTX, None), check_vma=False
+    )

time: 76.4 us -> 69.2 us (0.906)
  blocking collectives: 57.3 us -> 50.2 us
    all_to_all x4, blocking collectives: 57.3 us -> 50.2 us  [exchange(): lax.all_to_all(values, axes, split_axis=0, concat_axis=0, tiled=True, axi...]
  transfers between devices with their start and end apart: 2 -> 2, of which waited for: 1 -> 1; matrix products, arithmetic and copies ran while one was open for 1% -> 1% of each run, Pallas kernels for 5% -> 6%
where the time goes in v7:
time: 69.2 us; the launch traced here: 69 us
  blocking collectives  50.2 us (73%)
  Pallas kernels  9.54 us (14%)
  starting transfers between devices  8.28 us (12%)
    all_to_all x4, blocking collectives, exchange(): lax.all_to_all(values, axes, split_axis=0, concat_axis=0, tiled=True, axi...  50.2 us
    pallas_call x6, Pallas kernels, call(): pl.pallas_call(body, out_shape=outs, in_specs=[pl.BlockSpec(memory_space=...  9.54 us
    ppermute x1, starting transfers between devices, per_device(): other = lax.ppermute(own, 'core', SWAP)  5.04 us
    ppermute x1, starting transfers between devices, per_device(): x2 = lax.ppermute(x, 'core', SWAP)  3.24 us
  transfers between devices with their start and end apart: 2, of which 1 were waited for; matrix products, arithmetic and copies ran while one was open for 1% of the time, Pallas kernels for 6%

profile of v7, /device:TPU:1, one launch (start us, length us, event | category | flops | bytes accessed | tf_op | source)
XLA Modules:
  0.0 69.0 jit_solution(15169172832827513477)
XLA Ops:
  0.0 3.2 %collective-permute-start = (bf16[640,768]{1,0:T(8,128)(2,1)}, bf16[640,768]{1,0:T(8,128)(2,1)S(1)}, u32[]{:S(2)}, u32[]{:S(2)}) collective-permute-start(bf16[640,768]{1,0:T(8,128)(2,1)} %bitcast.13), channel_id=1, source_target_pairs={{0,8},{8,0},{1,9},{9,1},{2,10},{10,2},{3,11},{11,3},{4,12},{12,4},... | collective-permute-start | bytes 2949128 | tf_op jit(solution)/shard_map/ppermute | solution.py:196
  3.2 0.0 slice-start
  3.2 2.7 %shard_map.46 = (bf16[768,512]{1,0:T(8,128)(2,1)S(1)}, bf16[768,512]{1,0:T(8,128)(2,1)S(1)}, bf16[640,768]{1,0:T(8,128)(2,1)S(1)}, f32[640,512]{1,0:T(8,128)S(1)}) custom-call(bf16[768,1024]{1,0:T(8,128)(2,1)} %q_hbm.1, bf16[640,768]{1,0:T(8,128)(2,1)} %bitcast.14), custom_call_target="tpu_custom_call" | custom-call | flops 1006632960 | bytes 5000000 | tf_op jit(solution)/shard_map/pallas_call | solution.py:28
  6.0 0.0 collective-permute-done.x2
  6.0 0.0 slice-start.1
  6.0 0.0 copy-start
  6.0 2.1 %shard_map.48 = bf16[16,208,128]{2,1,0:T(8,128)(2,1)S(1)} custom-call(bf16[768,512]{1,0:T(8,128)(2,1)S(1)} %get-tuple-element.15.own_q, bf16[640,768]{1,0:T(8,128)(2,1)S(1)} %get-tuple-element.11.x, bf16[640,768]{1,0:T(8,128)(2,1)S(1)} %collective-permute-done.x2, f32[640,512]{1,0:T(8,128)S(1)} %get-tuple-element.13.logits), custom_call_target="tpu_custom_call" | custom-call | flops 1509949440 | bytes 5000000 | tf_op jit(solution)/shard_map/pallas_call | solution.py:28
  8.2 16.6 %all_to_all.20.parts = bf16[16,208,128]{2,1,0:T(8,128)(2,1)S(1)} all-to-all(bf16[16,208,128]{2,1,0:T(8,128)(2,1)S(1)} %shard_map.48), channel_id=1, replica_groups={{160,176,128,144,224,240,192,208,32,48,0,16,96,112,64,80},{168,184,136,..., dimensions={0} | all-to-all | bytes 1703936 | tf_op jit(solution)/shard_map/all_to_all | solution.py:183
  24.8 0.4 shard_map.49
  25.2 11.4 %all_to_all.21.received = bf16[8,4,768]{2,1,0:T(4,128)(2,1)S(1)} all-to-all(bf16[8,4,768]{2,1,0:T(4,128)(2,1)S(1)} %shard_map.49), channel_id=1, replica_groups={{4,5,6,7,0,1,2,3},{12,13,14,15,8,9,10,11},{20,21,22,23,16,17,18,19},{28..., dimensions={0} | all-to-all | bytes 98304 | tf_op jit(solution)/shard_map/all_to_all | solution.py:183
  36.6 0.0 slice-done
  36.6 0.0 slice-done.1
  36.6 0.0 copy-done
  36.6 1.8 %shard_map.50 = bf16[8,4,768]{2,1,0:T(4,128)(2,1)S(1)} custom-call(bf16[8,4,768]{2,1,0:T(4,128)(2,1)S(1)} %all_to_all.21.received, bf16[768,3072]{1,0:T(8,128)(2,1)S(1)} %bitcast.9, bf16[3072,768]{1,0:T(8,128)(2,1)S(1)} %bitcast.10), custom_call_target="tpu_custom_call" | custom-call | flops 301989888 | bytes 9500000 | tf_op jit(solution)/shard_map/pallas_call | solution.py:28
  38.4 9.5 %all_to_all.22 = bf16[8,4,768]{2,1,0:T(4,128)(2,1)S(1)} all-to-all(bf16[8,4,768]{2,1,0:T(4,128)(2,1)S(1)} %shard_map.50), channel_id=1, replica_groups={{4,5,6,7,0,1,2,3},{12,13,14,15,8,9,10,11},{20,21,22,23,16,17,18,19},{28..., dimensions={0} | all-to-all | bytes 98304 | tf_op jit(solution)/shard_map/all_to_all | solution.py:183
  47.9 0.1 broadcast_in_dim.11
  48.0 12.6 %all_to_all.23 = bf16[16,32,768]{2,1,0:T(8,128)(2,1)S(1)} all-to-all(bf16[16,32,768]{2,1,0:T(8,128)(2,1)S(1)} %broadcast_in_dim.11), channel_id=1, replica_groups={{160,176,128,144,224,240,192,208,32,48,0,16,96,112,64,80},{168,184,136,..., dimensions={0} | all-to-all | bytes 1572864 | tf_op jit(solution)/shard_map/all_to_all | solution.py:183
  60.6 5.0 %collective-permute-start.1 = (bf16[512,768]{1,0:T(8,128)(2,1)S(1)}, bf16[512,768]{1,0:T(8,128)(2,1)S(1)}, u32[]{:S(2)}, u32[]{:S(2)}) collective-permute-start(bf16[512,768]{1,0:T(8,128)(2,1)S(1)} %bitcast.11), channel_id=1, source_target_pairs={{0,8},{8,0},{1,9},{9,1},{2,10},{10,2},{3,11},{11,3},{4,12},{12,4},... | collective-permute-start | bytes 2359304 | tf_op jit(solution)/shard_map/ppermute | solution.py:240
  65.7 1.1 %shard_map.47 = (bf16[640,512]{1,0:T(8,128)(2,1)S(1)}, bf16[640,512]{1,0:T(8,128)(2,1)S(1)}) custom-call(bf16[640,768]{1,0:T(8,128)(2,1)S(1)} %get-tuple-element.11.x, bf16[768,512]{1,0:T(8,128)(2,1)S(1)} %get-tuple-element.12.other_q, f32[640,512]{1,0:T(8,128)S(1)} %get-tuple-element.13.logits), custom_call_target="tpu_custom_call" | custom-call | flops 503316480 | bytes 4000000 | tf_op jit(solution)/shard_map/pallas_call | solution.py:28
  66.8 0.7 fusion.partial
  67.5 0.1 collective-permute-done.1.rows
  67.6 1.4 %shard_map.51 = bf16[640,768]{1,0:T(8,128)(2,1)} custom-call(f32[640,768]{1,0:T(8,128)S(1)} %fusion.partial, bf16[640,512]{1,0:T(8,128)(2,1)S(1)} %get-tuple-element.16.weights, bf16[512,768]{1,0:T(8,128)(2,1)S(1)} %collective-permute-done.1.rows), custom_call_target="tpu_custom_call" | custom-call | flops 503316480 | bytes 4000000 | tf_op jit(solution)/shard_map/pallas_call | solution.py:28
  (2 shorter events, 0.0 us)
Async XLA Ops:
  0.0 6.0 %collective-permute-start = (bf16[640,768]{1,0:T(8,128)(2,1)}, bf16[640,768]{1,0:T(8,128)(2,1)S(1)}, u32[]{:S(2)}, u32[]{:S(2)}) collective-permute-start(bf16[640,768]{1,0:T(8,128)(2,1)} %bitcast.13), channel_id=1, source_target_pairs={{0,8},{8,0},{1,9},{9,1},{2,10},{10,2},{3,11},{11,3},{4,12},{12,4},... | collective-permute-start | bytes 2949128 | tf_op jit(solution)/shard_map/ppermute | solution.py:196
  3.2 33.3 %slice-start = ((s8[4718592]{0:T(1024)(128)(4,1)}), s8[4194304]{0:T(1024)(128)(4,1)S(1)}, s32[]{:S(2)}) async-start(s8[4718592]{0:T(1024)(128)(4,1)} %bitcast.7), calls=%async_computation.4 | async-start | bytes 8388608
  6.0 30.6 %slice-start.1 = ((s8[4718592]{0:T(1024)(128)(4,1)}), s8[524288]{0:T(1024)(128)(4,1)S(1)}, s32[]{:S(2)}) async-start(s8[4718592]{0:T(1024)(128)(4,1)} %bitcast.7), calls=%async_computation.5 | async-start | bytes 1048576
  6.0 30.6 %copy-start = (bf16[1,3072,768]{2,1,0:T(8,128)(2,1)S(1)}, bf16[1,3072,768]{2,1,0:T(8,128)(2,1)}, u32[]{:S(2)}) copy-start(bf16[1,3072,768]{2,1,0:T(8,128)(2,1)} %param.7) | copy-start | bytes 14155780
  60.6 7.0 %collective-permute-start.1 = (bf16[512,768]{1,0:T(8,128)(2,1)S(1)}, bf16[512,768]{1,0:T(8,128)(2,1)S(1)}, u32[]{:S(2)}, u32[]{:S(2)}) collective-permute-start(bf16[512,768]{1,0:T(8,128)(2,1)S(1)} %bitcast.11), channel_id=1, source_target_pairs={{0,8},{8,0},{1,9},{9,1},{2,10},{10,2},{3,11},{11,3},{4,12},{12,4},... | collective-permute-start | bytes 2359304 | tf_op jit(solution)/shard_map/ppermute | solution.py:240

commit v8 on v7

--- a/solution.py
+++ b/solution.py
@@ -40,7 +40,7 @@
     return jnp.max(logits, axis=0, keepdims=True).astype(BF16).astype(F32)
 
 
-def logit_kernel(slot_rows, turn, q_hbm, x_hbm, own_q, other_q, x, logits, q, sems):
+def logit_kernel(slot_rows, turn, q_hbm, x_hbm, own_q, q, pick_other, x, logits, sems):
     group = 256
     kept = group // 2
     chunk = q.shape[0] // CHUNKS
@@ -61,15 +61,15 @@
     chip = (column // slot_rows + TURN_Y) % (kept // slot_rows)
     place = chip * pair + (column + turn) % slot_rows + (kind ^ core) * slot_rows
     pick = jnp.where(row == place, 1.0, 0.0).astype(BF16)
+    pick_other[...] = pick[:, kept:]
     for load, rows in zip(loads, chunks):
         load.wait()
         blocks = q.shape[1] // group
         for b in range(blocks):
-            picked = dot(q[rows, b * group : (b + 1) * group], pick).astype(BF16)
+            picked = dot(q[rows, b * group : (b + 1) * group], pick[:, :kept]).astype(BF16)
             place = (b - TURN_X) % blocks
             columns = slice(place * kept, (place + 1) * kept)
-            own_q[rows, columns] = picked[:, :kept]
-            other_q[rows, columns] = picked[:, kept:]
+            own_q[rows, columns] = picked
     loads[CHUNKS].wait()
     logits[...] = dot(x[...], own_q[...])
 
@@ -107,9 +107,15 @@
         out[c, rows - TAIL :, :] = stats[:, group : group + LANES]
 
 
-def softmax_kernel(x, other_q, logits, own_w, other_w):
+def softmax_kernel(x, q, pick, logits, own_w, other_w):
     own = logits[...]
-    other = dot(x[...], other_q[...])
+    group, kept = pick.shape
+    blocks = q.shape[1] // group
+    parts = []
+    for place in range(blocks):
+        b = (place + TURN_X) % blocks
+        parts.append(dot(q[:, b * group : (b + 1) * group], pick[...]).astype(BF16))
+    other = dot(x[...], jnp.concatenate(parts, axis=1))
     top = jnp.maximum(jnp.max(own, axis=1, keepdims=True), jnp.max(other, axis=1, keepdims=True))
     own = jnp.exp(own - top)
     other = jnp.exp(other - top)
@@ -195,17 +201,18 @@
     slot_rows = half // chips
     x2 = lax.ppermute(x, "core", SWAP)
     shape = jax.ShapeDtypeStruct
-    own_q, other_q, kept, logits = call(
+    own_q, query, pick, kept, logits = call(
         functools.partial(logit_kernel, slot_rows, slot_rows // grp_count * TURN_Z),
         [
             shape((width, half), BF16),
-            shape((width, half), BF16),
+            shape((width, slots), BF16),
+            shape((2 * LANES, LANES), BF16),
             shape((count, width), BF16),
             shape((count, half), F32),
         ],
         2 * slots * width * count, 5_000_000,
         [pltpu.with_memory_space_constraint(a, pltpu.HBM) for a in (slot_query, x)],
-        [pltpu.VMEM((width, slots), BF16), pltpu.SemaphoreType.DMA((CHUNKS + 1,))],
+        [pltpu.SemaphoreType.DMA((CHUNKS + 1,))],
         pl.ANY,
     )
     (packed,) = call(
@@ -241,7 +248,7 @@
     own_w, other_w = call(
         softmax_kernel,
         [shape((count, half), BF16), shape((count, half), BF16)],
-        slots * width * count, 4_000_000, (kept, other_q, logits),
+        slots * width * count, 4_000_000, (kept, query, pick, logits),
     )
     (mixed,) = call(
         final_kernel,

time: 69.2 us -> 70.6 us (1.020)
  local copies, waits for them, and re-layouts: 0.11 us -> 1.05 us
    unnamed x6 -> x10, local copies, waits for them, and re-layouts: 0.02 us -> 0.96 us
  transfers between devices with their start and end apart: 2 -> 2, of which waited for: 1 -> 0; matrix products, arithmetic and copies ran while one was open for 1% -> 1% of each run, Pallas kernels for 6% -> 6%
where the time goes in v8:
time: 70.6 us; the launch traced here: 70.4 us
  blocking collectives  50.3 us (71%)
  Pallas kernels  9.97 us (14%)
  starting transfers between devices  8.28 us (12%)
  local copies, waits for them, and re-layouts  1.05 us (1%)
    all_to_all x4, blocking collectives, exchange(): lax.all_to_all(values, axes, split_axis=0, concat_axis=0, tiled=True, axi...  50.3 us
    pallas_call x6, Pallas kernels, call(): pl.pallas_call(body, out_shape=outs, in_specs=[pl.BlockSpec(memory_space=...  9.97 us
    ppermute x1, starting transfers between devices, per_device(): other = lax.ppermute(own, 'core', SWAP)  5.04 us
    ppermute x1, starting transfers between devices, per_device(): x2 = lax.ppermute(x, 'core', SWAP)  3.24 us
  transfers between devices with their start and end apart: 2, of which 0 were waited for; matrix products, arithmetic and copies ran while one was open for 1% of the time, Pallas kernels for 6%

profile of v8, /device:TPU:1, one launch (start us, length us, event | category | flops | bytes accessed | tf_op | source)
XLA Modules:
  0.0 70.4 jit_solution(7745819465887991745)
XLA Ops:
  0.0 3.2 %collective-permute-start = (bf16[640,768]{1,0:T(8,128)(2,1)}, bf16[640,768]{1,0:T(8,128)(2,1)S(1)}, u32[]{:S(2)}, u32[]{:S(2)}) collective-permute-start(bf16[640,768]{1,0:T(8,128)(2,1)} %bitcast.13), channel_id=1, source_target_pairs={{0,8},{8,0},{1,9},{9,1},{2,10},{10,2},{3,11},{11,3},{4,12},{12,4},... | collective-permute-start | bytes 2949128 | tf_op jit(solution)/shard_map/ppermute | solution.py:202
  3.2 0.0 slice-start
  3.2 2.7 %shard_map.46 = (bf16[768,512]{1,0:T(8,128)(2,1)S(1)}, bf16[768,1024]{1,0:T(8,128)(2,1)S(1)}, bf16[256,128]{1,0:T(8,128)(2,1)S(1)}, bf16[640,768]{1,0:T(8,128)(2,1)S(1)}, f32[640,512]{1,0:T(8,128)S(1)}) custom-call(bf16[768,1024]{1,0:T(8,128)(2,1)} %q_hbm.1, bf16[640,768]{1,0:T(8,128)(2,1)} %bitcast.14), custom_call_target="tpu_custom_call" | custom-call | flops 1006632960 | bytes 5000000 | tf_op jit(solution)/shard_map/pallas_call | solution.py:28
  6.0 0.0 collective-permute-done.x2
  6.0 0.0 slice-start.1
  6.0 0.0 copy-start
  6.0 2.1 %shard_map.48 = bf16[16,208,128]{2,1,0:T(8,128)(2,1)S(1)} custom-call(bf16[768,512]{1,0:T(8,128)(2,1)S(1)} %get-tuple-element.17.own_q, bf16[640,768]{1,0:T(8,128)(2,1)S(1)} %get-tuple-element.12.x, bf16[640,768]{1,0:T(8,128)(2,1)S(1)} %collective-permute-done.x2, f32[640,512]{1,0:T(8,128)S(1)} %get-tuple-element.15.logits), custom_call_target="tpu_custom_call" | custom-call | flops 1509949440 | bytes 5000000 | tf_op jit(solution)/shard_map/pallas_call | solution.py:28
  8.2 0.0 copy-start.1
  8.2 0.9 %copy-done.1 = bf16[640,768]{1,0:T(8,128)(2,1)} copy-done((bf16[640,768]{1,0:T(8,128)(2,1)}, bf16[640,768]{1,0:T(8,128)(2,1)S(1)}, u32[]{:S(2)}) %copy-start.1) | copy-done | bytes 983064
  9.1 16.6 %all_to_all.20.parts = bf16[16,208,128]{2,1,0:T(8,128)(2,1)S(1)} all-to-all(bf16[16,208,128]{2,1,0:T(8,128)(2,1)S(1)} %shard_map.48), channel_id=1, replica_groups={{160,176,128,144,224,240,192,208,32,48,0,16,96,112,64,80},{168,184,136,..., dimensions={0} | all-to-all | bytes 1703936 | tf_op jit(solution)/shard_map/all_to_all | solution.py:189
  25.7 0.4 shard_map.49
  26.1 11.4 %all_to_all.21.received = bf16[8,4,768]{2,1,0:T(4,128)(2,1)S(1)} all-to-all(bf16[8,4,768]{2,1,0:T(4,128)(2,1)S(1)} %shard_map.49), channel_id=1, replica_groups={{4,5,6,7,0,1,2,3},{12,13,14,15,8,9,10,11},{20,21,22,23,16,17,18,19},{28..., dimensions={0} | all-to-all | bytes 98304 | tf_op jit(solution)/shard_map/all_to_all | solution.py:189
  37.5 0.0 slice-done
  37.5 0.0 slice-done.1
  37.5 0.0 copy-done
  37.5 1.8 %shard_map.50 = bf16[8,4,768]{2,1,0:T(4,128)(2,1)S(1)} custom-call(bf16[8,4,768]{2,1,0:T(4,128)(2,1)S(1)} %all_to_all.21.received, bf16[768,3072]{1,0:T(8,128)(2,1)S(1)} %bitcast.9, bf16[3072,768]{1,0:T(8,128)(2,1)S(1)} %bitcast.10), custom_call_target="tpu_custom_call" | custom-call | flops 301989888 | bytes 9500000 | tf_op jit(solution)/shard_map/pallas_call | solution.py:28
  39.3 9.5 %all_to_all.22 = bf16[8,4,768]{2,1,0:T(4,128)(2,1)S(1)} all-to-all(bf16[8,4,768]{2,1,0:T(4,128)(2,1)S(1)} %shard_map.50), channel_id=1, replica_groups={{4,5,6,7,0,1,2,3},{12,13,14,15,8,9,10,11},{20,21,22,23,16,17,18,19},{28..., dimensions={0} | all-to-all | bytes 98304 | tf_op jit(solution)/shard_map/all_to_all | solution.py:189
  48.9 0.0 copy-start.2
  48.9 0.1 broadcast_in_dim.11
  49.0 12.7 %all_to_all.23 = bf16[16,32,768]{2,1,0:T(8,128)(2,1)S(1)} all-to-all(bf16[16,32,768]{2,1,0:T(8,128)(2,1)S(1)} %broadcast_in_dim.11), channel_id=1, replica_groups={{160,176,128,144,224,240,192,208,32,48,0,16,96,112,64,80},{168,184,136,..., dimensions={0} | all-to-all | bytes 1572864 | tf_op jit(solution)/shard_map/all_to_all | solution.py:189
  61.7 5.0 %collective-permute-start.1 = (bf16[512,768]{1,0:T(8,128)(2,1)S(1)}, bf16[512,768]{1,0:T(8,128)(2,1)S(1)}, u32[]{:S(2)}, u32[]{:S(2)}) collective-permute-start(bf16[512,768]{1,0:T(8,128)(2,1)S(1)} %bitcast.11), channel_id=1, source_target_pairs={{0,8},{8,0},{1,9},{9,1},{2,10},{10,2},{3,11},{11,3},{4,12},{12,4},... | collective-permute-start | bytes 2359304 | tf_op jit(solution)/shard_map/ppermute | solution.py:247
  66.8 0.0 copy-done.2
  66.8 1.5 %shard_map.47 = (bf16[640,512]{1,0:T(8,128)(2,1)S(1)}, bf16[640,512]{1,0:T(8,128)(2,1)S(1)}) custom-call(bf16[640,768]{1,0:T(8,128)(2,1)S(1)} %copy-done.2, bf16[768,1024]{1,0:T(8,128)(2,1)S(1)} %get-tuple-element.13.q, bf16[256,128]{1,0:T(8,128)(2,1)S(1)} %get-tuple-element.14.pick, f32[640,512]{1,0:T(8,128)S(1)} %get-tuple-element.15.logits), custom_call_target="tpu_custom_call" | custom-call | flops 503316480 | bytes 4000000 | tf_op jit(solution)/shard_map/pallas_call | solution.py:28
  68.3 0.7 fusion.partial
  69.0 0.0 collective-permute-done.1.rows
  69.0 1.4 %shard_map.51 = bf16[640,768]{1,0:T(8,128)(2,1)} custom-call(f32[640,768]{1,0:T(8,128)S(1)} %fusion.partial, bf16[640,512]{1,0:T(8,128)(2,1)S(1)} %get-tuple-element.18.weights, bf16[512,768]{1,0:T(8,128)(2,1)S(1)} %collective-permute-done.1.rows), custom_call_target="tpu_custom_call" | custom-call | flops 503316480 | bytes 4000000 | tf_op jit(solution)/shard_map/pallas_call | solution.py:28
  (2 shorter events, 0.0 us)
Async XLA Ops:
  0.0 6.0 %collective-permute-start = (bf16[640,768]{1,0:T(8,128)(2,1)}, bf16[640,768]{1,0:T(8,128)(2,1)S(1)}, u32[]{:S(2)}, u32[]{:S(2)}) collective-permute-start(bf16[640,768]{1,0:T(8,128)(2,1)} %bitcast.13), channel_id=1, source_target_pairs={{0,8},{8,0},{1,9},{9,1},{2,10},{10,2},{3,11},{11,3},{4,12},{12,4},... | collective-permute-start | bytes 2949128 | tf_op jit(solution)/shard_map/ppermute | solution.py:202
  3.2 34.3 %slice-start = ((s8[4718592]{0:T(1024)(128)(4,1)}), s8[4194304]{0:T(1024)(128)(4,1)S(1)}, s32[]{:S(2)}) async-start(s8[4718592]{0:T(1024)(128)(4,1)} %bitcast.7), calls=%async_computation.4 | async-start | bytes 8388608
  6.0 31.6 %slice-start.1 = ((s8[4718592]{0:T(1024)(128)(4,1)}), s8[524288]{0:T(1024)(128)(4,1)S(1)}, s32[]{:S(2)}) async-start(s8[4718592]{0:T(1024)(128)(4,1)} %bitcast.7), calls=%async_computation.5 | async-start | bytes 1048576
  6.0 31.5 %copy-start = (bf16[1,3072,768]{2,1,0:T(8,128)(2,1)S(1)}, bf16[1,3072,768]{2,1,0:T(8,128)(2,1)}, u32[]{:S(2)}) copy-start(bf16[1,3072,768]{2,1,0:T(8,128)(2,1)} %param.7) | copy-start | bytes 14155780
  8.2 0.9 %copy-start.1 = (bf16[640,768]{1,0:T(8,128)(2,1)}, bf16[640,768]{1,0:T(8,128)(2,1)S(1)}, u32[]{:S(2)}) copy-start(bf16[640,768]{1,0:T(8,128)(2,1)S(1)} %get-tuple-element.12.x) | copy-start | bytes 2949124
  48.9 17.9 %copy-start.2 = (bf16[640,768]{1,0:T(8,128)(2,1)S(1)}, bf16[640,768]{1,0:T(8,128)(2,1)}, u32[]{:S(2)}) copy-start(bf16[640,768]{1,0:T(8,128)(2,1)} %copy-done.1) | copy-start | bytes 2949124
  61.7 7.3 %collective-permute-start.1 = (bf16[512,768]{1,0:T(8,128)(2,1)S(1)}, bf16[512,768]{1,0:T(8,128)(2,1)S(1)}, u32[]{:S(2)}, u32[]{:S(2)}) collective-permute-start(bf16[512,768]{1,0:T(8,128)(2,1)S(1)} %bitcast.11), channel_id=1, source_target_pairs={{0,8},{8,0},{1,9},{9,1},{2,10},{10,2},{3,11},{11,3},{4,12},{12,4},... | collective-permute-start | bytes 2359304 | tf_op jit(solution)/shard_map/ppermute | solution.py:247

commit v9 on v7

--- a/solution.py
+++ b/solution.py
@@ -16,7 +16,7 @@
 TAIL = 16
 CHUNKS = 2
 PIECES = 4
-TURN_X, TURN_Y, TURN_Z = 2, 2, 4
+TURN_X, TURN_Y, TURN_Z = 2, 2, 5
 OVER_ROWS = (((0,), (0,)), ((), ()))
 
 

time: 69.2 us -> 69.2 us (level)
  no operation moved by 1% of the time
where the time goes in v9:
time: 69.2 us; the launch traced here: 68.9 us
  blocking collectives  50.2 us (73%)
  Pallas kernels  9.54 us (14%)
  starting transfers between devices  8.2 us (12%)
    all_to_all x4, blocking collectives, exchange(): lax.all_to_all(values, axes, split_axis=0, concat_axis=0, tiled=True, axi...  50.2 us
    pallas_call x6, Pallas kernels, call(): pl.pallas_call(body, out_shape=outs, in_specs=[pl.BlockSpec(memory_space=...  9.54 us
    ppermute x1, starting transfers between devices, per_device(): other = lax.ppermute(own, 'core', SWAP)  4.96 us
    ppermute x1, starting transfers between devices, per_device(): x2 = lax.ppermute(x, 'core', SWAP)  3.24 us
  transfers between devices with their start and end apart: 2, of which 1 were waited for; matrix products, arithmetic and copies ran while one was open for 1% of the time, Pallas kernels for 6%

profile of v9, /device:TPU:1, one launch (start us, length us, event | category | flops | bytes accessed | tf_op | source)
XLA Modules:
  0.0 68.9 jit_solution(9149134311533770775)
XLA Ops:
  0.0 3.2 %collective-permute-start = (bf16[640,768]{1,0:T(8,128)(2,1)}, bf16[640,768]{1,0:T(8,128)(2,1)S(1)}, u32[]{:S(2)}, u32[]{:S(2)}) collective-permute-start(bf16[640,768]{1,0:T(8,128)(2,1)} %bitcast.13), channel_id=1, source_target_pairs={{0,8},{8,0},{1,9},{9,1},{2,10},{10,2},{3,11},{11,3},{4,12},{12,4},... | collective-permute-start | bytes 2949128 | tf_op jit(solution)/shard_map/ppermute | solution.py:196
  3.2 0.0 slice-start
  3.2 2.7 %shard_map.46 = (bf16[768,512]{1,0:T(8,128)(2,1)S(1)}, bf16[768,512]{1,0:T(8,128)(2,1)S(1)}, bf16[640,768]{1,0:T(8,128)(2,1)S(1)}, f32[640,512]{1,0:T(8,128)S(1)}) custom-call(bf16[768,1024]{1,0:T(8,128)(2,1)} %q_hbm.1, bf16[640,768]{1,0:T(8,128)(2,1)} %bitcast.14), custom_call_target="tpu_custom_call" | custom-call | flops 1006632960 | bytes 5000000 | tf_op jit(solution)/shard_map/pallas_call | solution.py:28
  6.0 0.0 collective-permute-done.x2
  6.0 0.0 slice-start.1
  6.0 0.0 copy-start
  6.0 2.1 %shard_map.48 = bf16[16,208,128]{2,1,0:T(8,128)(2,1)S(1)} custom-call(bf16[768,512]{1,0:T(8,128)(2,1)S(1)} %get-tuple-element.15.own_q, bf16[640,768]{1,0:T(8,128)(2,1)S(1)} %get-tuple-element.11.x, bf16[640,768]{1,0:T(8,128)(2,1)S(1)} %collective-permute-done.x2, f32[640,512]{1,0:T(8,128)S(1)} %get-tuple-element.13.logits), custom_call_target="tpu_custom_call" | custom-call | flops 1509949440 | bytes 5000000 | tf_op jit(solution)/shard_map/pallas_call | solution.py:28
  8.2 16.6 %all_to_all.20.parts = bf16[16,208,128]{2,1,0:T(8,128)(2,1)S(1)} all-to-all(bf16[16,208,128]{2,1,0:T(8,128)(2,1)S(1)} %shard_map.48), channel_id=1, replica_groups={{160,176,128,144,224,240,192,208,32,48,0,16,96,112,64,80},{168,184,136,..., dimensions={0} | all-to-all | bytes 1703936 | tf_op jit(solution)/shard_map/all_to_all | solution.py:183
  24.8 0.4 shard_map.49
  25.2 11.7 %all_to_all.21.received = bf16[8,4,768]{2,1,0:T(4,128)(2,1)S(1)} all-to-all(bf16[8,4,768]{2,1,0:T(4,128)(2,1)S(1)} %shard_map.49), channel_id=1, replica_groups={{5,6,7,0,1,2,3,4},{13,14,15,8,9,10,11,12},{21,22,23,16,17,18,19,20},{29..., dimensions={0} | all-to-all | bytes 98304 | tf_op jit(solution)/shard_map/all_to_all | solution.py:183
  36.8 0.0 slice-done
  36.8 0.0 slice-done.1
  36.9 0.0 copy-done
  36.9 1.8 %shard_map.50 = bf16[8,4,768]{2,1,0:T(4,128)(2,1)S(1)} custom-call(bf16[8,4,768]{2,1,0:T(4,128)(2,1)S(1)} %all_to_all.21.received, bf16[768,3072]{1,0:T(8,128)(2,1)S(1)} %bitcast.9, bf16[3072,768]{1,0:T(8,128)(2,1)S(1)} %bitcast.10), custom_call_target="tpu_custom_call" | custom-call | flops 301989888 | bytes 9500000 | tf_op jit(solution)/shard_map/pallas_call | solution.py:28
  38.6 9.2 %all_to_all.22 = bf16[8,4,768]{2,1,0:T(4,128)(2,1)S(1)} all-to-all(bf16[8,4,768]{2,1,0:T(4,128)(2,1)S(1)} %shard_map.50), channel_id=1, replica_groups={{5,6,7,0,1,2,3,4},{13,14,15,8,9,10,11,12},{21,22,23,16,17,18,19,20},{29..., dimensions={0} | all-to-all | bytes 98304 | tf_op jit(solution)/shard_map/all_to_all | solution.py:183
  47.8 0.1 broadcast_in_dim.11
  47.9 12.7 %all_to_all.23 = bf16[16,32,768]{2,1,0:T(8,128)(2,1)S(1)} all-to-all(bf16[16,32,768]{2,1,0:T(8,128)(2,1)S(1)} %broadcast_in_dim.11), channel_id=1, replica_groups={{160,176,128,144,224,240,192,208,32,48,0,16,96,112,64,80},{168,184,136,..., dimensions={0} | all-to-all | bytes 1572864 | tf_op jit(solution)/shard_map/all_to_all | solution.py:183
  60.7 5.0 %collective-permute-start.1 = (bf16[512,768]{1,0:T(8,128)(2,1)S(1)}, bf16[512,768]{1,0:T(8,128)(2,1)S(1)}, u32[]{:S(2)}, u32[]{:S(2)}) collective-permute-start(bf16[512,768]{1,0:T(8,128)(2,1)S(1)} %bitcast.11), channel_id=1, source_target_pairs={{0,8},{8,0},{1,9},{9,1},{2,10},{10,2},{3,11},{11,3},{4,12},{12,4},... | collective-permute-start | bytes 2359304 | tf_op jit(solution)/shard_map/ppermute | solution.py:240
  65.6 1.1 %shard_map.47 = (bf16[640,512]{1,0:T(8,128)(2,1)S(1)}, bf16[640,512]{1,0:T(8,128)(2,1)S(1)}) custom-call(bf16[640,768]{1,0:T(8,128)(2,1)S(1)} %get-tuple-element.11.x, bf16[768,512]{1,0:T(8,128)(2,1)S(1)} %get-tuple-element.12.other_q, f32[640,512]{1,0:T(8,128)S(1)} %get-tuple-element.13.logits), custom_call_target="tpu_custom_call" | custom-call | flops 503316480 | bytes 4000000 | tf_op jit(solution)/shard_map/pallas_call | solution.py:28
  66.7 0.7 fusion.partial
  67.4 0.1 collective-permute-done.1.rows
  67.5 1.4 %shard_map.51 = bf16[640,768]{1,0:T(8,128)(2,1)} custom-call(f32[640,768]{1,0:T(8,128)S(1)} %fusion.partial, bf16[640,512]{1,0:T(8,128)(2,1)S(1)} %get-tuple-element.16.weights, bf16[512,768]{1,0:T(8,128)(2,1)S(1)} %collective-permute-done.1.rows), custom_call_target="tpu_custom_call" | custom-call | flops 503316480 | bytes 4000000 | tf_op jit(solution)/shard_map/pallas_call | solution.py:28
  (2 shorter events, 0.0 us)
Async XLA Ops:
  0.0 6.0 %collective-permute-start = (bf16[640,768]{1,0:T(8,128)(2,1)}, bf16[640,768]{1,0:T(8,128)(2,1)S(1)}, u32[]{:S(2)}, u32[]{:S(2)}) collective-permute-start(bf16[640,768]{1,0:T(8,128)(2,1)} %bitcast.13), channel_id=1, source_target_pairs={{0,8},{8,0},{1,9},{9,1},{2,10},{10,2},{3,11},{11,3},{4,12},{12,4},... | collective-permute-start | bytes 2949128 | tf_op jit(solution)/shard_map/ppermute | solution.py:196
  3.2 33.6 %slice-start = ((s8[4718592]{0:T(1024)(128)(4,1)}), s8[4194304]{0:T(1024)(128)(4,1)S(1)}, s32[]{:S(2)}) async-start(s8[4718592]{0:T(1024)(128)(4,1)} %bitcast.7), calls=%async_computation.4 | async-start | bytes 8388608
  6.0 30.9 %slice-start.1 = ((s8[4718592]{0:T(1024)(128)(4,1)}), s8[524288]{0:T(1024)(128)(4,1)S(1)}, s32[]{:S(2)}) async-start(s8[4718592]{0:T(1024)(128)(4,1)} %bitcast.7), calls=%async_computation.5 | async-start | bytes 1048576
  6.0 30.9 %copy-start = (bf16[1,3072,768]{2,1,0:T(8,128)(2,1)S(1)}, bf16[1,3072,768]{2,1,0:T(8,128)(2,1)}, u32[]{:S(2)}) copy-start(bf16[1,3072,768]{2,1,0:T(8,128)(2,1)} %param.7) | copy-start | bytes 14155780
  60.7 6.9 %collective-permute-start.1 = (bf16[512,768]{1,0:T(8,128)(2,1)S(1)}, bf16[512,768]{1,0:T(8,128)(2,1)S(1)}, u32[]{:S(2)}, u32[]{:S(2)}) collective-permute-start(bf16[512,768]{1,0:T(8,128)(2,1)S(1)} %bitcast.11), channel_id=1, source_target_pairs={{0,8},{8,0},{1,9},{9,1},{2,10},{10,2},{3,11},{11,3},{4,12},{12,4},... | collective-permute-start | bytes 2359304 | tf_op jit(solution)/shard_map/ppermute | solution.py:240
